TPU v7x, 32 devices: a whole 2x2x4 slice. The times are simulated.
32 devices in a mesh: slab: 8 (over y, x, core), grp: 4 (over z).
Axes of the slice: x: 2, y: 2, z: 4, core: 2. Of those that a mesh axis runs over, the one named last changes fastest.
Arguments:
- source: float32 [3, 256, 2048], P(None, 'slab', 'grp'), may hold values from -8 to 8
- conductivity: float32 [3, 256, 2048], P(None, 'slab', 'grp'), may hold values from 0.1 to 10
- leakance: float32 [2, 256, 2048], P(None, 'slab', 'grp'), may hold values from 0.05 to 5
- storage: float32 [3, 256, 2048], P(None, 'slab', 'grp'), may hold values from 0.1 to 1
- et_rate: float32 [256, 2048], P('slab', 'grp'), may hold values from 0.05 to 1
- zone_of_block: int32 [32, 256], P('slab', 'grp'), may hold values from 0 to 255
- zone_recharge: float32 [256], replicated, may hold values from -4 to 4
- zone_weight: float32 [256], replicated, may hold values from 0.25 to 4
- pair_zones: int32 [512, 2], replicated, may hold values from 0 to 255, as said below
- pair_weight: float32 [512], replicated, may hold values from 0.25 to 4
Outputs:
- solution: float32 [3, 256, 2048], P(None, 'slab', 'grp')
- residual: float32 [3, 256, 2048], P(None, 'slab', 'grp')
Inputs may be any that keep to these rules, and one draw needn't show every extreme that they name: `pair_zones`: each row names two different zones; every zone is the first entry of some row.
All inputs are finite; a program needn't handle non-finite values.
Results may differ from a plain program's by a relative error of at most 0.00017.
Values sent between devices are 32-bit elements; how exact they have to be, the bound alone decides.
No kernel may reach another device: no remote copies, remote signals or barrier semaphores. Data moves between devices by JAX's collectives and lax.ppermute only.
A program may use at most 64 MiB of HBM per device.

v0:
```python
import math
from types import SimpleNamespace

import jax
import jax.numpy as jnp
import numpy as np
from jax import lax
from jax.experimental import pallas as pl
from jax.experimental.pallas import tpu as pltpu
from jax.sharding import PartitionSpec as P

COUPLE = 4.0
PRECOND_T = 2.0
PRECOND_SHIFT = 3.0
HIGHEST = lax.Precision.HIGHEST
BOTH = ("slab", "grp")
VMEM_LIMIT = 64 * 1024 * 1024
F32, BF16 = jnp.float32, jnp.bfloat16


def sine_basis(count):
    index = np.arange(1, count + 1)
    basis = math.sqrt(2.0 / (count + 1)) * np.sin(np.pi * np.outer(index, index) / (count + 1))
    return basis, 4.0 * np.sin(np.pi * index / (2.0 * (count + 1))) ** 2


def fourier_basis(count):
    cells = np.arange(count)[:, None]
    waves = np.concatenate([np.arange(count // 2 + 1), np.arange(1, count // 2)])[None, :]
    turned = 2.0 * np.pi * ((cells * waves) % count) / count
    is_sine = np.arange(count)[None, :] > count // 2
    basis = np.where(is_sine, np.sin(turned), np.cos(turned)) * math.sqrt(2.0 / count)
    basis[:, 0] /= math.sqrt(2.0)
    basis[:, count // 2] /= math.sqrt(2.0)
    return basis, 4.0 * np.sin(np.pi * waves[0] / count) ** 2


def chain_tables(cross, total, block):
    half = (PRECOND_SHIFT / PRECOND_T + cross) / 2.0 + 1.0
    decay = 1.0 / (half + np.sqrt(half * half - 1.0))
    scale = 1.0 / ((1.0 - decay**total) * PRECOND_T * (1.0 / decay - decay))

    def green(distance):
        distance = distance % total
        return PRECOND_T * scale * (decay**distance + decay ** (total - distance))

    count = total // block
    tables = np.zeros((4, count, len(cross)))
    for back in range(count):
        tables[0, back] = green(block * back)
        tables[1, back] = green(block * (back - 1) - 1) + (1.0 if back == 1 % count else 0.0)
        tables[2, back] = green(block * (back + 1) + 1) + (1.0 if back == count - 1 else 0.0)
        tables[3, back] = green(block * back)
    return tables


def grid_tables(slabs, groups, rows, cols):
    rows_total, cols_total = slabs * rows, groups * cols
    sine_rows, cross_rows = sine_basis(rows)
    sine_cols, cross_cols = sine_basis(cols)
    waves, cross_waves = fourier_basis(rows_total)
    weight = 1.0 / (PRECOND_SHIFT + PRECOND_T * (cross_rows[:, None] + cross_cols[None, :]))
    wave_weight = 1.0 / (PRECOND_SHIFT + PRECOND_T * (cross_waves[:, None] + cross_cols[None, :]))
    first, last = sine_cols[0], sine_cols[-1]
    answer = np.zeros((2, cols, 128))
    for end, row in enumerate((0, rows - 1)):
        inside = PRECOND_T * np.einsum("ri,ij,i->jr", sine_rows, weight, sine_rows[:, row])
        answer[end, :, :rows] = first[:, None] * inside
        answer[end, :, rows : 2 * rows] = last[:, None] * inside
    spread_rows = np.repeat(np.eye(rows // 8), 8, axis=0)
    spread_cols = np.repeat(np.eye(cols // 8), 8, axis=0)
    mode_rows, mode_cols = sine_rows @ spread_rows, sine_cols @ spread_cols
    mixed = np.einsum("ri,ij,ib->rbj", sine_rows, weight, mode_rows)
    coarse = np.zeros((rows // 8, cols // 8, 2 * cols + 128))
    coarse[:, :, :cols] = np.einsum("bj,jc->bcj", mixed[0], mode_cols)
    coarse[:, :, cols : 2 * cols] = np.einsum("bj,jc->bcj", mixed[-1], mode_cols)
    coarse[:, :, 2 * cols : 2 * cols + rows] = np.einsum("rbj,j,jc->bcr", mixed, first, mode_cols)
    coarse[:, :, 2 * cols + rows : 2 * cols + 2 * rows] = np.einsum(
        "rbj,j,jc->bcr", mixed, last, mode_cols
    )
    column_chain = chain_tables(cross_waves, cols_total, cols)
    tile = max(8, groups)
    own_columns = np.zeros((groups, 4, tile, rows_total))
    for group in range(groups):
        for other in range(groups):
            own_columns[group, :, other] = column_chain[:, (group - other) % groups]
    around = np.zeros((slabs, 8, rows_total))
    for slab in range(slabs):
        around[slab, 0] = waves[(rows * slab - 1) % rows_total]
        around[slab, 1] = waves[(rows * slab + rows) % rows_total]
    ends = np.zeros((8, cols))
    ends[0], ends[1] = first, last
    blocks = (rows // 8) * (cols // 8)
    down = np.tile(spread_cols, (1, rows // 8))
    exact = dict(
        weight=weight,
        row_chain=chain_tables(cross_cols, rows_total, rows).reshape(4 * slabs, cols),
        own_columns=own_columns.reshape(groups, 4 * tile, rows_total),
        around=around,
        ends=ends,
        place=np.tile(np.eye(cols // 8), (1, rows // 8)),
    )
    split = dict(
        sine_rows=sine_rows,
        sine_cols=sine_cols,
        answer=answer.reshape(2 * cols, 128),
        coarse=coarse.reshape(blocks, 2 * cols + 128),
        waves=waves,
        wave_weight=wave_weight,
        up_modes=down.T @ sine_cols,
    )
    tables = {name: np.asarray(table, np.float32) for name, table in exact.items()}
    for name, table in split.items():
        high = table.astype(jnp.bfloat16)
        tables[name] = np.stack([high, (table - high.astype(np.float64)).astype(jnp.bfloat16)])
    tables["down"] = down.astype(jnp.bfloat16)
    return tables


def terms(value, count):
    parts = []
    for _ in range(count):
        part = value.astype(BF16).astype(F32)
        parts.append(part)
        value = value - part
    return parts


DIMS = (((1,), (0,)), ((), ()))
DIMS_T = (((1,), (1,)), ((), ()))


def product(left, right, dims):
    return lax.dot_general(left, right, dims, preferred_element_type=F32)


def mm(value, table, dims=DIMS):
    rows = value.shape[0]
    high, low = terms(value, 2)
    both = product(jnp.concatenate([high, low], axis=0).astype(BF16), table[0], dims)
    return both[:rows] + both[rows:] + product(high.astype(BF16), table[1], dims)


def mm_left(table, value, dims=DIMS):
    rows = table[0].shape[0]
    high, low = terms(value, 2)
    both = product(jnp.concatenate([table[0], table[1]], axis=0), high.astype(BF16), dims)
    return both[:rows] + both[rows:] + product(table[0], low.astype(BF16), dims)


def mm_exact(value, table, dims=DIMS):
    rows = value.shape[0]
    every = product(jnp.concatenate(terms(value, 3), axis=0).astype(BF16), table, dims)
    return every[:rows] + every[rows : 2 * rows] + every[2 * rows :]


def mm_f32(left, right, dims=DIMS):
    return lax.dot_general(left, right, dims, precision=HIGHEST, preferred_element_type=F32)


def iota(shape, dim):
    return lax.broadcasted_iota(jnp.int32, shape, dim)


def lookup(values, index):
    rows, lanes = index.shape
    zones = values.shape[1]
    within, which = index & 127, index >> 7
    pieces = []
    for start in range(0, lanes, 128):
        part = jnp.zeros((rows, 128), F32)
        for half in range(zones // 128):
            table = jnp.broadcast_to(values[:, 128 * half : 128 * (half + 1)], (rows, 128))
            found = jnp.take_along_axis(table, within[:, start : start + 128], axis=1)
            part = jnp.where(which[:, start : start + 128] == half, found, part)
        pieces.append(part)
    return jnp.concatenate(pieces, axis=1) if len(pieces) > 1 else pieces[0]


def rings(q_mixed, t):
    sine_rows = t.sine_rows
    inside = mm_left(sine_rows, mm_left(sine_rows, q_mixed) * t.weight[...])
    rows = inside.shape[0]
    ends = t.ends
    left = jnp.sum(inside * ends[0:1], axis=1, keepdims=True)
    right = jnp.sum(inside * ends[1:2], axis=1, keepdims=True)
    return inside[0:1], inside[rows - 1 : rows], left, right


def side_lanes(parts, last=None):
    rows, cols = parts[0].shape
    lane = iota((rows, 128), 1)
    tall = [jnp.where(lane == 127, p[:, cols - 128 :], p[:, :128]) for p in parts]
    if last is not None:
        tall.append(jnp.where(lane == 127, last[1], last[0]))
    while len(tall) < 4:
        tall.append(jnp.zeros((rows, 128), F32))
    turned = jnp.concatenate(tall, axis=0).T
    return turned[0:1], turned[127:128]


def stencil(values, before, after, left, right):
    rows, cols = values.shape
    row, col = iota(values.shape, 0), iota(values.shape, 1)
    up = jnp.where(row == 0, before, pltpu.roll(values, 1, 0))
    down = jnp.where(row == rows - 1, after, pltpu.roll(values, rows - 1, 0))
    west = jnp.where(col == 0, left, pltpu.roll(values, 1, 1))
    east = jnp.where(col == cols - 1, right, pltpu.roll(values, cols - 1, 1))
    return (up + down) + (west + east)


def to_line(spread, block_cols):
    own = iota(spread.shape, 1) // block_cols == iota(spread.shape, 0)
    return jnp.sum(jnp.where(own, spread, 0.0), axis=0, keepdims=True)


def zone_totals(surface, zone_line, down, zones):
    rows, cols = surface.shape
    sums = [jnp.sum(surface[8 * i : 8 * i + 8], axis=0, keepdims=True) for i in range(rows // 8)]
    sums = jnp.concatenate(sums + [jnp.zeros((8 - rows // 8, cols), F32)], axis=0)
    line = to_line(mm_exact(sums, down), cols // 8)
    blocks = zone_line.shape[1]
    hot = (iota((zones, blocks), 0) == zone_line.astype(jnp.int32)).astype(F32).astype(BF16)
    line = jnp.broadcast_to(line, (8, blocks))
    return mm_exact(line, hot, DIMS_T)[0:1]


def field_rows(lines, down, block_rows, block_cols):
    row, place = iota((8, lines[0][0].shape[1]), 0), iota((8, lines[0][0].shape[1]), 1) // block_cols
    picked = jnp.zeros(row.shape, F32)
    for index, (line, wanted) in enumerate(lines):
        picked = jnp.where((row == index) & (place == wanted), line, picked)
    return mm_exact(picked, down, DIMS_T), picked


def spread_rows8(lines, rows):
    return jnp.concatenate(
        [jnp.broadcast_to(lines[i : i + 1], (8, lines.shape[1])) for i in range(rows // 8)], axis=0
    )


def smooth(first_rows, last_rows, edges, q_mixed, slab, group, groups, t):
    devices = first_rows.shape[0]
    slabs = devices // groups
    rows, cols = q_mixed.shape
    before = jnp.zeros_like(first_rows)
    after = jnp.zeros_like(first_rows)
    chain = t.row_chain
    for back in range(slabs):
        turned_first = pltpu.roll(first_rows, groups * back, 0) if back else first_rows
        turned_last = pltpu.roll(last_rows, groups * back, 0) if back else last_rows
        line = [chain[slabs * kind + back : slabs * kind + back + 1] for kind in range(4)]
        before = before + (line[0] * turned_first + line[1] * turned_last)
        after = after + (line[2] * turned_first + line[3] * turned_last)
    mine = iota(before.shape, 0) == slab * groups + group
    own_before = jnp.sum(jnp.where(mine, before, 0.0), axis=0, keepdims=True)
    own_after = jnp.sum(jnp.where(mine, after, 0.0), axis=0, keepdims=True)
    answer = t.answer
    edges = edges + mm(jnp.concatenate([before, after], axis=1), answer)
    tile, per = max(8, groups), 128 // rows
    lane = iota(edges.shape, 1) // rows
    lines = []
    for side in range(2):
        joined = jnp.zeros_like(edges)
        for i in range(per):
            moved = pltpu.roll(edges, rows * (i - side) % 128, 1) if i != side else edges
            moved = pltpu.roll(moved, devices - groups * i, 0) if i else moved
            joined = jnp.where(lane == i, moved, joined)
        step = per * groups
        lines.append(jnp.concatenate([joined[step * p : step * p + tile] for p in range(slabs // per)], axis=1))
    waves = t.waves
    waved = mm(jnp.concatenate(lines, axis=0), waves)
    count = waved.shape[1]
    firsts, lasts = waved[:tile], waved[tile:]
    chain = t.own_columns
    table = [chain[tile * kind : tile * (kind + 1)] for kind in range(4)]
    left = jnp.sum(table[0] * firsts + table[1] * lasts, axis=0, keepdims=True)
    right = jnp.sum(table[2] * firsts + table[3] * lasts, axis=0, keepdims=True)
    row = iota((8, count), 0)
    sides = jnp.where(row == 0, left, jnp.where(row == 1, right, 0.0))
    own_rows = pl.ds(pl.multiple_of(slab * rows, rows), rows)
    columns = mm_left([waves[0, own_rows, :], waves[1, own_rows, :]], sides, DIMS_T)
    left_col, right_col = columns[:, 0:1], columns[:, 1:2]
    around = t.around
    north, south = around[0:1], around[1:2]
    four = jnp.where(
        row == 0,
        north * left,
        jnp.where(row == 1, north * right, jnp.where(row == 2, south * left, jnp.where(row == 3, south * right, 0.0))),
    )
    four = mm(four, t.wave_weight)
    ends = t.ends
    first, last = ends[0:1], ends[1:2]
    north_row = own_before + PRECOND_T * (first * four[0:1] + last * four[1:2])
    south_row = own_after + PRECOND_T * (first * four[2:3] + last * four[3:4])
    place = iota((rows, cols), 0)
    loaded = q_mixed + PRECOND_T * (
        jnp.where(place == 0, north_row, 0.0)
        + jnp.where(place == rows - 1, south_row, 0.0)
        + left_col * first
        + right_col * last
    )
    sine_rows = t.sine_rows
    inside = mm_left(sine_rows, mm_left(sine_rows, loaded) * t.weight[...])
    pad = jnp.zeros((6, cols), F32)
    whole = mm(jnp.concatenate([inside, north_row, south_row, pad], axis=0), t.sine_cols)
    return whole[:rows], whole[rows : rows + 1], whole[rows + 1 : rows + 2], left_col, right_col


class Operands:
    def __init__(self, copies, buffers):
        self._copies, self._buffers = copies, buffers

    def __getattr__(self, name):
        if name in self._copies:
            self._copies.pop(name).wait()
        return self._buffers[name]


def call(body, ins, outs):
    names, results = list(ins), list(outs)
    pairs = [value if isinstance(value, tuple) else (value, ()) for value in ins.values()]
    arrays = [array for array, _ in pairs]
    copied = [place for place, (_, part) in enumerate(pairs) if part is not None]

    def shape_of(array, part):
        if isinstance(part, str):
            return array.shape[1:]
        return tuple(len(range(*cut.indices(size))) for cut, size in zip(part, array.shape)) + array.shape[len(part) :]

    def kernel(*refs):
        given, refs = refs[: len(names)], refs[len(names) :]
        made, refs = refs[: len(results)], refs[len(results) :]
        held, refs = refs[: len(copied)], refs[len(copied) :]
        built, (in_sems, out_sems) = refs[: len(results)], refs[len(results) :]
        copies = {}
        for slot, place in enumerate(copied):
            part = pairs[place][1]
            origin = given[place].at[lax.axis_index(part) if isinstance(part, str) else part] if part else given[place]
            copies[names[place]] = pltpu.make_async_copy(origin, held[slot], in_sems.at[slot])
            copies[names[place]].start()
        sent = []

        def done(*buffers):
            for buffer in buffers:
                place = [other is buffer for other in built].index(True)
                sent.append(pltpu.make_async_copy(buffer, made[place], out_sems.at[place]))
                sent[-1].start()

        get = Operands(copies, {names[place]: buffer for place, buffer in zip(copied, held)})
        body(get, SimpleNamespace(**dict(zip(results, built))), done)
        for place in copied:
            getattr(get, names[place])
        assert len(sent) == len(results)
        for copy in sent:
            copy.wait()

    buffers = [pltpu.VMEM(shape_of(*pairs[place]), arrays[place].dtype) for place in copied]
    made = pl.pallas_call(
        kernel,
        out_shape=[jax.ShapeDtypeStruct(outs[name], F32) for name in results],
        in_specs=[pl.BlockSpec(memory_space=pl.ANY)] * len(names),
        out_specs=[pl.BlockSpec(memory_space=pl.ANY)] * len(results),
        scratch_shapes=buffers
        + [pltpu.VMEM(outs[name], F32) for name in results]
        + [pltpu.SemaphoreType.DMA((len(copied),)), pltpu.SemaphoreType.DMA((len(results),))],
        compiler_params=pltpu.CompilerParams(vmem_limit_bytes=VMEM_LIMIT),
    )(*arrays)
    return SimpleNamespace(**dict(zip(results, made)))


def shards(
    source,
    conductivity,
    leakance,
    storage,
    et_rate,
    zone_of_block,
    zone_recharge,
    zone_weight,
    pair_zones,
    pair_weight,
):
    slabs, groups = lax.axis_size("slab"), lax.axis_size("grp")
    layers, rows, cols = source.shape
    devices = slabs * groups
    zones = zone_weight.shape[0]
    tables = {name: jnp.asarray(table) for name, table in grid_tables(slabs, groups, rows, cols).items()}
    t = SimpleNamespace(**tables)
    t.own_columns, t.around = (t.own_columns, "grp"), (t.around, "slab")
    block_rows, block_cols = rows // 8, cols // 8
    blocks = block_rows * block_cols
    at_zones = 2 * cols
    at_sides = at_zones + blocks
    widths = (at_sides + 5 * 128, at_zones + zones + 2 * 128)
    area = (layers, rows, cols)

    def neighbours(first, last):
        return (
            lax.ppermute(last, "slab", [(i, i + 1) for i in range(slabs - 1)]),
            lax.ppermute(first, "slab", [(i + 1, i) for i in range(slabs - 1)]),
        )

    def exchange(chunk):
        return lax.all_to_all(chunk, BOTH, split_axis=0, concat_axis=0, tiled=True)

    def start_body(get, out, done):
        ids = get.zone_of_block[...].astype(F32)
        ids = jnp.concatenate([ids, jnp.zeros((8 - block_rows, block_cols), F32)], axis=0)
        zone_line = to_line(mm_f32(ids, get.place[...]), block_cols)
        index = jnp.broadcast_to(zone_line, (8, blocks)).astype(jnp.int32)
        found = lookup(get.zone_recharge[...], index)[0:1]
        field, _ = field_rows([(found, i) for i in range(block_rows)], get.down[...], block_rows, block_cols)
        source_ref, rhs = get.source, out.rhs
        rhs[0] = source_ref[0] + spread_rows8(field, rows)
        for layer in range(1, layers):
            rhs[layer] = source_ref[layer]
        done(out.rhs)
        total = rhs[0]
        for layer in range(1, layers):
            total = total + rhs[layer]
        q_mixed = mm(total, get.sine_cols)
        out.q_mixed[...] = q_mixed
        done(out.q_mixed)
        cond, store, leak = get.conductivity, get.storage, get.leakance
        partial, halo = out.partial, (out.first, out.last)
        for layer in range(layers):
            own = cond[layer]
            diagonal = store[layer] + 0.5 * (4.0 * own + stencil(own, 0.0, 0.0, 0.0, 0.0))
            if layer < layers - 1:
                diagonal = diagonal + leak[layer]
            if layer > 0:
                diagonal = diagonal + leak[layer - 1]
            if layer == 0:
                diagonal = diagonal + get.et_rate[...]
            partial[layer] = diagonal
            for end, row in enumerate((0, rows - 1)):
                halo[end][layer : layer + 1] = own[row : row + 1]
                halo[end][layers + layer : layers + layer + 1] = diagonal[row : row + 1]
                halo[end][2 * layers + layer : 2 * layers + layer + 1] = rhs[layer, row : row + 1]
        done(out.partial, out.first, out.last)
        first, last, left, right = rings(q_mixed, get)
        line, chunk = out.line, out.chunk
        line[:, :cols] = first
        line[:, cols : 2 * cols] = last
        line[:, at_zones:at_sides] = zone_line
        west, east = side_lanes([rhs[layer] for layer in range(layers)], (left, right))
        line[:, at_sides : at_sides + 128] = west
        line[:, at_sides + 128 : at_sides + 256] = east
        west, east = side_lanes(
            [cond[layer] for layer in range(layers)], (partial[0, :, 0:1], partial[0, :, cols - 1 : cols])
        )
        line[:, at_sides + 256 : at_sides + 384] = west
        line[:, at_sides + 384 : at_sides + 512] = east
        west, east = side_lanes([partial[layer] for layer in range(1, layers)])
        line[:, at_sides + 512 :] = jnp.where(iota((1, 128), 1) < 64, west, pltpu.roll(east, 64, 1))
        chunk[...] = jnp.broadcast_to(line[...][None], chunk.shape)
        done(out.chunk, out.line)

    started = call(
        start_body,
        dict(
            zone_of_block=zone_of_block,
            zone_recharge=zone_recharge[None],
            place=t.place,
            down=t.down,
            source=source,
            sine_cols=t.sine_cols,
            conductivity=conductivity,
            storage=storage,
            leakance=leakance,
            et_rate=et_rate,
            sine_rows=t.sine_rows,
            weight=t.weight,
            ends=t.ends,
        ),
        dict(
            rhs=area,
            q_mixed=(rows, cols),
            partial=area,
            first=(3 * layers, cols),
            last=(3 * layers, cols),
            line=(1, widths[0]),
            chunk=(devices, 1, widths[0]),
        ),
    )
    rhs = started.rhs
    received = first_received = exchange(started.chunk)
    halo_north, halo_south = neighbours(started.first, started.last)
    first_north, first_south = halo_north, halo_south

    def couple_body(get, out, done):
        ids, weights = get.pair_zones, get.pair_weight
        place = iota((zones, ids.shape[1]), 0)
        table = (place == ids[0:1]).astype(F32) - (place == ids[1:2]).astype(F32)
        matrix = mm_f32(table * weights[...], table, DIMS_T)
        own = iota((zones, zones), 0) == iota((zones, zones), 1)
        matrix = matrix + jnp.where(own, get.zone_weight[...], 0.0)
        out.couple[...] = (COUPLE * zones / (slabs * rows * groups * cols)) * matrix
        done(out.couple)

    couple = call(
        couple_body,
        dict(pair_zones=pair_zones.T, pair_weight=pair_weight[None], zone_weight=zone_weight[None]),
        dict(couple=(zones, zones)),
    ).couple

    def step_body(number, get, out, done):
        coupled, final = number > 0, number == 2
        slab, group = lax.axis_index("slab"), lax.axis_index("grp")
        own = slab * groups + group
        has_north = (slab > 0).astype(F32)
        has_south = (slab < slabs - 1).astype(F32)
        has_west = (group > 0).astype(F32)
        has_east = (group < groups - 1).astype(F32)
        recv = get.received

        def of(shift, start):
            return recv[pl.ds(jnp.clip(own + shift, 0, devices - 1), 1), 0, start : start + 128]

        first_rows, last_rows = recv[:, 0, :cols], recv[:, 0, cols : 2 * cols]
        sides_at = at_sides if not coupled else at_zones + zones
        lane = iota((devices, 128), 1)
        edges = jnp.where(
            lane < rows,
            pltpu.roll(recv[:, 0, sides_at : sides_at + 128], rows, 1),
            pltpu.roll(recv[:, 0, sides_at + 128 : sides_at + 256], 2 * rows, 1),
        )
        edges = jnp.where(lane < 2 * rows, edges, 0.0)
        q_in = get.q_mixed[...]
        w_ref = get.w
        surface = w_ref[0]
        if coupled:
            totals = jnp.sum(recv[:, 0, at_zones : at_zones + zones], axis=0, keepdims=True)
            reply = mm_f32(jnp.broadcast_to(totals, (8, zones)), get.couple[...])[0:1]
            every = lookup(reply, get.zone_map[:, 0, :].astype(jnp.int32))
            coarse = mm(every, get.coarse)
            first_rows = first_rows + coarse[:, :cols]
            last_rows = last_rows + coarse[:, cols : 2 * cols]
            edges = edges + coarse[:, 2 * cols :]
            device = iota(every.shape, 0)
            line_of = lambda shift: jnp.sum(
                jnp.where(device == own + shift, every, 0.0), axis=0, keepdims=True
            )
            mine = line_of(0)
            wanted = [(mine, i) for i in range(block_rows)]
            wanted += [(line_of(-groups), block_rows - 1), (line_of(groups), 0)]
            field, picked = field_rows(wanted, get.down[...], block_rows, block_cols)
            modes = mm(picked, get.up_modes)
            q_in = q_in + spread_rows8(modes, rows)
            surface = surface + spread_rows8(field, rows)
            column = iota((rows, blocks), 1)
            base = block_cols * (iota((rows, blocks), 0) // 8)
            west_value = jnp.sum(
                jnp.where(column == base + block_cols - 1, line_of(-1), 0.0), axis=1, keepdims=True
            )
            east_value = jnp.sum(jnp.where(column == base, line_of(1), 0.0), axis=1, keepdims=True)
        if final:
            out.w[0] = surface
            for layer in range(1, layers):
                out.w[layer] = w_ref[layer]
            done(out.w)
        elif coupled:
            out.w[0] = surface
            for layer in range(1, layers):
                out.w[layer] = w_ref[layer]
            done(out.w)
        s, s_north, s_south, s_west, s_east = smooth(
            first_rows, last_rows, edges, q_in, slab, group, groups, get
        )
        cond, leak = get.conductivity, get.leakance
        north_ref, south_ref = get.north, get.south
        row, col = iota((rows, cols), 0), iota((rows, cols), 1)
        if coupled:
            cond_north, cond_south = get.first_north, get.first_south
            sides = get.sides
            lanes = [of(-1, sides_at + 128), of(1, sides_at)]
            diagonal_ref, inverse_ref = get.diagonal, get.inverse
            beside = get.beside
        else:
            cond_north, cond_south = north_ref, south_ref
            lanes = [of(-1, sides_at + 128), of(1, sides_at)]
            lanes += [of(-1, sides_at + 384) * has_west, of(1, sides_at + 256) * has_east]
            lanes += [of(-1, sides_at + 512), of(1, sides_at + 512)]
            diagonal_ref, inverse_ref, sides, beside = out.diagonal, out.inverse, out.sides, out.beside
        turned = jnp.concatenate(lanes + [jnp.zeros((128 - len(lanes), 128), F32)], axis=0).T
        if not coupled:
            corner = [
                of(-groups - 1, sides_at + 384) * (has_north * has_west),
                of(-groups + 1, sides_at + 256) * (has_north * has_east),
                of(groups - 1, sides_at + 384) * (has_south * has_west),
                of(groups + 1, sides_at + 256) * (has_south * has_east),
            ]
            ghosts = []
            partial = get.partial
            line_col, line_row = iota((1, cols), 1), iota((rows, 1), 0)
            for layer in range(layers):
                c_north, c_south = north_ref[layer : layer + 1], south_ref[layer : layer + 1]
                c_west = turned[rows * layer : rows * (layer + 1), 2:3]
                c_east = turned[rows * layer : rows * (layer + 1), 3:4]
                both = jnp.where(lane[:rows] == 0, c_west, jnp.where(lane[:rows] == 1, c_east, 0.0))
                sides[layer] = both
                diagonal = partial[layer] + 0.5 * (
                    jnp.where(row == 0, c_north, 0.0)
                    + jnp.where(row == rows - 1, c_south, 0.0)
                    + jnp.where(col == 0, c_west, 0.0)
                    + jnp.where(col == cols - 1, c_east, 0.0)
                )
                diagonal_ref[layer] = diagonal
                inverse_ref[layer] = 1.0 / diagonal
                start, end = rows * layer, rows * layer + rows - 1
                nw, ne = corner[0][:, end : end + 1], corner[1][:, end : end + 1]
                sw, se = corner[2][:, start : start + 1], corner[3][:, start : start + 1]
                own_cond = cond[layer]
                d_north = north_ref[layers + layer : layers + layer + 1] + 0.5 * (
                    own_cond[0:1] + jnp.where(line_col == 0, nw, jnp.where(line_col == cols - 1, ne, 0.0))
                )
                d_south = south_ref[layers + layer : layers + layer + 1] + 0.5 * (
                    own_cond[rows - 1 : rows]
                    + jnp.where(line_col == 0, sw, jnp.where(line_col == cols - 1, se, 0.0))
                )
                if layer == 0:
                    west, east = turned[3 * rows : 4 * rows, 2:3], turned[3 * rows : 4 * rows, 3:4]
                else:
                    west = turned[64 + rows * (layer - 1) : 64 + rows * layer, 4:5]
                    east = turned[rows * (layer - 1) : rows * layer, 5:6]
                d_west = west + 0.5 * (
                    own_cond[:, 0:1] + jnp.where(line_row == 0, nw, jnp.where(line_row == rows - 1, sw, 0.0))
                )
                d_east = east + 0.5 * (
                    own_cond[:, cols - 1 : cols]
                    + jnp.where(line_row == 0, ne, jnp.where(line_row == rows - 1, se, 0.0))
                )
                ghosts.append((1.0 / d_north, 1.0 / d_south, 1.0 / d_west, 1.0 / d_east))
            sides[layers] = jnp.where(lane[:rows] == 0, ghosts[0][2], jnp.where(lane[:rows] == 1, ghosts[0][3], 0.0))
            beside[0:1] = ghosts[0][0]
            beside[1:2] = ghosts[0][1]
            done(out.diagonal, out.inverse, out.sides, out.beside)
        v_out, image_out = out.v, out.image
        fields, outside = [], []
        for layer in range(layers):
            value = (surface if layer == 0 else w_ref[layer]) * inverse_ref[layer] + s
            v_out[layer] = value
            fields.append(value)
            west = turned[rows * layer : rows * (layer + 1), 0:1]
            east = turned[rows * layer : rows * (layer + 1), 1:2]
            if coupled:
                north, south = north_ref[layer : layer + 1], south_ref[layer : layer + 1]
                if layer == 0:
                    north = north + beside[0:1] * field[block_rows : block_rows + 1]
                    south = south + beside[1:2] * field[block_rows + 1 : block_rows + 2]
                    west = west + sides[layers, :, 0:1] * west_value
                    east = east + sides[layers, :, 1:2] * east_value
            else:
                near = ghosts[layer]
                place = 2 * layers + layer
                north, south = north_ref[place : place + 1] * near[0], south_ref[place : place + 1] * near[1]
                west, east = west * near[2], east * near[3]
            outside.append(
                (
                    (north + s_north) * has_north,
                    (south + s_south) * has_south,
                    (west + s_west) * has_west,
                    (east + s_east) * has_east,
                )
            )
        done(out.v)
        images = []
        for layer in range(layers):
            value, own_cond = fields[layer], cond[layer]
            north, south, west, east = outside[layer]
            plain = stencil(value, north, south, west, east)
            carried = stencil(
                value * own_cond,
                north * cond_north[layer : layer + 1],
                south * cond_south[layer : layer + 1],
                west * sides[layer, :, 0:1],
                east * sides[layer, :, 1:2],
            )
            image = diagonal_ref[layer] * value - 0.5 * (own_cond * plain + carried)
            if layer < layers - 1:
                image = image - leak[layer] * fields[layer + 1]
            if layer > 0:
                image = image - leak[layer - 1] * fields[layer - 1]
            image_out[layer] = image
            images.append(image)
        done(out.image)
        line, chunk = out.line, out.chunk
        totals = zone_totals(fields[0], get.zone_line[:, at_zones:at_sides], get.down[...], zones)
        if final:
            rhs_ref, v0_ref, v1_ref, w0_ref = get.rhs, get.v0, get.v1, get.w0

            def dot(left, right):
                total = left[0] * right[0]
                for layer in range(1, layers):
                    total = total + left[layer] * right[layer]
                return jnp.sum(jnp.sum(total, axis=0, keepdims=True), axis=1, keepdims=True)

            w1 = [surface] + [w_ref[layer] for layer in range(1, layers)]
            products = [
                dot(v0_ref, w0_ref), dot(v0_ref, w1), dot(v1_ref, w1), dot(fields, w0_ref), dot(fields, w1),
                dot(fields, images), dot(v0_ref, rhs_ref), dot(v1_ref, rhs_ref), dot(fields, rhs_ref),
            ]
            packed = jnp.zeros((1, 128), F32)
            for place, value in enumerate(products):
                packed = jnp.where(iota((1, 128), 1) == place, value, packed)
            line[:, :zones] = totals
            line[:, zones:] = packed
        else:
            depth = images[0]
            for layer in range(1, layers):
                depth = depth + images[layer]
            q_next = mm(depth, get.sine_cols)
            out.q_mixed[...] = q_next
            done(out.q_mixed)
            scaled = [images[layer] * inverse_ref[layer] for layer in range(layers)]
            for layer in range(layers):
                out.first[layer : layer + 1] = scaled[layer][0:1]
                out.last[layer : layer + 1] = scaled[layer][rows - 1 : rows]
            done(out.first, out.last)
            first, last, left, right = rings(q_next, get)
            west, east = side_lanes(scaled, (left, right))
            line[:, :cols] = first
            line[:, cols : 2 * cols] = last
            line[:, at_zones : at_zones + zones] = totals
            line[:, at_zones + zones : at_zones + zones + 128] = west
            line[:, at_zones + zones + 128 :] = east
        chunk[...] = jnp.broadcast_to(line[...][None], chunk.shape)
        done(out.chunk, out.line)

    tail_width = zones + 128
    shared = {}

    def step(number, received, q_mixed, w, north, south, more=()):
        ins = dict(received=received)
        if number > 0:
            ins |= dict(couple=couple, zone_map=zone_map, coarse=t.coarse)
        ins |= dict(row_chain=t.row_chain, answer=t.answer, q_mixed=q_mixed, w=w, down=t.down)
        if number > 0:
            ins |= dict(up_modes=t.up_modes)
        ins |= dict(waves=t.waves, own_columns=t.own_columns, around=t.around, wave_weight=t.wave_weight)
        ins |= dict(ends=t.ends, sine_rows=t.sine_rows, weight=t.weight, sine_cols=t.sine_cols)
        ins |= dict(north=north, south=south, conductivity=conductivity, leakance=leakance)
        ins |= dict(zone_line=started.line)
        outs = dict(v=area, image=area)
        if number > 0:
            ins |= dict(first_north=first_north, first_south=first_south) | shared
            outs |= dict(w=area)
        else:
            ins |= dict(partial=started.partial, couple=(couple, None))
            outs |= dict(diagonal=area, inverse=area, sides=(layers + 1, rows, 128), beside=(2, cols))
        ins |= dict(more)
        if number == 2:
            outs |= dict(line=(1, tail_width), chunk=(devices, 1, tail_width))
        else:
            outs |= dict(
                q_mixed=(rows, cols), first=(layers, cols), last=(layers, cols), line=(1, widths[1]), chunk=(devices, 1, widths[1])
            )
        return call(lambda get, out, done: step_body(number, get, out, done), ins, outs)

    one = step(0, received, started.q_mixed, rhs, halo_north, halo_south)
    shared.update(diagonal=one.diagonal, inverse=one.inverse, sides=one.sides, beside=one.beside)
    zone_map = (first_received, (slice(None), slice(None), slice(at_zones, at_sides)))
    received = exchange(one.chunk)
    halo_north, halo_south = neighbours(one.first, one.last)
    two = step(1, received, one.q_mixed, one.image, halo_north, halo_south)
    received = exchange(two.chunk)
    halo_north, halo_south = neighbours(two.first, two.last)
    more = dict(rhs=rhs, v0=one.v, v1=two.v, w0=two.w)
    three = step(2, received, two.q_mixed, two.image, halo_north, halo_south, more)
    received = exchange(three.chunk)

    def finish_body(get, out, done):
        sums = jnp.sum(get.received[:, 0, :], axis=0, keepdims=True)
        totals = sums[:, :zones]
        reply = mm_f32(jnp.broadcast_to(totals, (8, zones)), get.couple[...])
        zone_line = get.zone_line[:, at_zones:at_sides]
        index = jnp.broadcast_to(zone_line, (8, blocks)).astype(jnp.int32)
        found = lookup(reply[0:1], index)[0:1]
        field, _ = field_rows([(found, i) for i in range(block_rows)], get.down[...], block_rows, block_cols)
        coupled = spread_rows8(field, rows)
        a00, a01, a11, a02, a12, a22, h0, h1, h2 = [sums[:, zones + i : zones + i + 1] for i in range(9)]
        a22 = a22 + jnp.sum(totals * reply[0:1], axis=1, keepdims=True)
        l10, l20 = a01 / a00, a02 / a00
        d1 = a11 - l10 * a01
        l21 = (a12 - l10 * a02) / d1
        d2 = a22 - l20 * a02 - l21 * (a12 - l10 * a02)
        y1 = h1 - l10 * h0
        y2 = h2 - l20 * h0 - l21 * y1
        c2 = y2 / d2
        c1 = y1 / d1 - l21 * c2
        c0 = h0 / a00 - l10 * c1 - l20 * c2
        v0, v1, v2, w0, w1, w2 = get.v0, get.v1, get.v2, get.w0, get.w1, get.w2
        rhs_ref = get.rhs
        for layer in range(layers):
            last = w2[layer] + coupled if layer == 0 else w2[layer]
            out.solution[layer] = c0 * v0[layer] + c1 * v1[layer] + c2 * v2[layer]
            out.residual[layer] = rhs_ref[layer] - c0 * w0[layer] - c1 * w1[layer] - c2 * last
        done(out.solution, out.residual)

    ended = call(
        finish_body,
        dict(received=received, couple=couple, zone_line=started.line, down=t.down)
        | dict(rhs=rhs, v0=one.v, v1=two.v, v2=three.v, w0=two.w, w1=three.w, w2=three.image),
        dict(solution=area, residual=area),
    )
    return ended.solution, ended.residual


def solution(mesh):
    placed = (
        P(None, "slab", "grp"),
        P(None, "slab", "grp"),
        P(None, "slab", "grp"),
        P(None, "slab", "grp"),
        P("slab", "grp"),
        P("slab", "grp"),
        P(),
        P(),
        P(),
        P(),
    )
    return jax.shard_map(
        shards,
        mesh=mesh,
        in_specs=placed,
        out_specs=(P(None, "slab", "grp"), P(None, "slab", "grp")),
        check_vma=False,
    )
```

profile of v0, /device:TPU:0, one launch (start us, length us, event | category | flops | bytes accessed | tf_op | source)
XLA Modules:
  0.0 84.6 jit_solution(14291955473084702033)
XLA Ops:
  0.6 3.5 %shard_map.239 = (f32[3,32,512]{2,1,0:T(8,128)}, f32[32,512]{1,0:T(8,128)}, f32[3,32,512]{2,1,0:T(8,128)}, f32[9,512]{1,0:T(8,128)}, f32[9,512]{1,0:T(8,128)}, /...) custom-call(s32[4,64]{1,0:T(4,128)} %refs_0_.1, f32[1,256]{1,0:T(1,128)} %bitcast.6, f32[64,256]{1,0:T(8,128)} %constant.33.clone.refs_2_, ...), custom_call_target="tpu_custom_call" | custom-call | tf_op jit(solution)/shard_map/pallas_call | solution.py:359
  4.1 7.4 %all-to-all-start = ((f32[32,1,1920]{2,1,0:T(1,128)}), f32[32,1,1920]{2,1,0:T(1,128)}, u32[]{:S(2)}, u32[]{:S(2)}) async-start(f32[32,1,1920]{2,1,0:T(1,128)} %get-tuple-element.30), calls=%async_computation | async-start | bytes 491520 | tf_op jit(solution)/shard_map/all_to_all | solution.py:405
  11.6 2.7 %collective-permute-start = (f32[9,512]{1,0:T(8,128)}, f32[9,512]{1,0:T(8,128)}, u32[]{:S(2)}, u32[]{:S(2)}) collective-permute-start(f32[9,512]{1,0:T(8,128)} %get-tuple-element.33), channel_id=1, source_target_pairs={{0,4},{4,8},{8,12},{12,16},{16,20},{20,24},{24,28},{1,5},{5,9},{9,... | collective-permute-start | bytes 55304 | tf_op jit(solution)/shard_map/ppermute | solution.py:400
  14.2 1.3 %collective-permute-start.1 = (f32[9,512]{1,0:T(8,128)}, f32[9,512]{1,0:T(8,128)}, u32[]{:S(2)}, u32[]{:S(2)}) collective-permute-start(f32[9,512]{1,0:T(8,128)} %get-tuple-element.34), channel_id=1, source_target_pairs={{4,0},{8,4},{12,8},{16,12},{20,16},{24,20},{28,24},{5,1},{9,5},{13... | collective-permute-start | bytes 55304 | tf_op jit(solution)/shard_map/ppermute | solution.py:401
  15.5 2.4 %shard_map.240.refs_20_.refs_1_ = f32[256,256]{1,0:T(8,128)} custom-call(s32[2,512]{1,0:T(2,128)} %bitcast.4, f32[1,512]{1,0:T(1,128)} %bitcast.5, f32[1,256]{1,0:T(1,128)} %bitcast.7), custom_call_target="tpu_custom_call" | custom-call | tf_op jit(solution)/shard_map/pallas_call | solution.py:359
  17.9 0.0 collective-permute-done.refs_14_.refs_23_
  17.9 0.3 collective-permute-done.1.refs_15_.refs_24_
  18.2 3.3 %all-to-all-done.refs_0_.refs_2_ = f32[32,1,1920]{2,1,0:T(1,128)} async-done(((f32[32,1,1920]{2,1,0:T(1,128)}), f32[32,1,1920]{2,1,0:T(1,128)}, u32[]{:S(2)}, u32[]{:S(2)}) %all-to-all-start) | async-done | bytes 245792 | tf_op jit(solution)/shard_map/all_to_all | solution.py:405
  21.5 5.7 %shard_map.241 = (f32[3,32,512]{2,1,0:T(8,128)}, f32[3,32,512]{2,1,0:T(8,128)}, f32[3,32,512]{2,1,0:T(8,128)}, f32[3,32,512]{2,1,0:T(8,128)}, f32[4,32,128]{2,1,...) custom-call(f32[32,1,1920]{2,1,0:T(1,128)} %all-to-all-done.refs_0_., ...), custom_call_target="tpu_custom_call" | custom-call | tf_op jit(solution)/shard_map/pallas_call | solution.py:359
  27.2 4.5 %all-to-all-start.1 = ((f32[32,1,1536]{2,1,0:T(1,128)}), f32[32,1,1536]{2,1,0:T(1,128)}, u32[]{:S(2)}, u32[]{:S(2)}) async-start(f32[32,1,1536]{2,1,0:T(1,128)} %get-tuple-element.37), calls=%async_computation.1 | async-start | bytes 393216 | tf_op jit(solution)/shard_map/all_to_all | solution.py:405
  31.8 2.7 %collective-permute-start.2 = (f32[3,512]{1,0:T(4,128)}, f32[3,512]{1,0:T(4,128)}, u32[]{:S(2)}, u32[]{:S(2)}) collective-permute-start(f32[3,512]{1,0:T(4,128)} %get-tuple-element.40), channel_id=1, source_target_pairs={{0,4},{4,8},{8,12},{12,16},{16,20},{20,24},{24,28},{1,5},{5,9},{9,... | collective-permute-start | bytes 18440 | tf_op jit(solution)/shard_map/ppermute | solution.py:400
  34.4 1.3 %collective-permute-start.3 = (f32[3,512]{1,0:T(4,128)}, f32[3,512]{1,0:T(4,128)}, u32[]{:S(2)}, u32[]{:S(2)}) collective-permute-start(f32[3,512]{1,0:T(4,128)} %get-tuple-element.41), channel_id=1, source_target_pairs={{4,0},{8,4},{12,8},{16,12},{20,16},{24,20},{28,24},{5,1},{9,5},{13... | collective-permute-start | bytes 18440 | tf_op jit(solution)/shard_map/ppermute | solution.py:401
  35.7 2.7 %collective-permute-done.3.refs_19_ = f32[3,512]{1,0:T(4,128)} collective-permute-done((f32[3,512]{1,0:T(4,128)}, f32[3,512]{1,0:T(4,128)}, u32[]{:S(2)}, u32[]{:S(2)}) %collective-permute-start.3) | collective-permute-done | bytes 6176 | tf_op jit(solution)/shard_map/ppermute | solution.py:401
  38.4 2.7 %all-to-all-done.1.refs_0_ = f32[32,1,1536]{2,1,0:T(1,128)} async-done(((f32[32,1,1536]{2,1,0:T(1,128)}), f32[32,1,1536]{2,1,0:T(1,128)}, u32[]{:S(2)}, u32[]{:S(2)}) %all-to-all-start.1) | async-done | bytes 196640 | tf_op jit(solution)/shard_map/all_to_all | solution.py:405
  41.1 7.2 %shard_map.242 = (f32[3,32,512]{2,1,0:T(8,128)}, f32[3,32,512]{2,1,0:T(8,128)}, f32[3,32,512]{2,1,0:T(8,128)}, f32[32,512]{1,0:T(8,128)}, f32[3,512]{1,0:T(4,128...) custom-call(f32[32,1,1536]{2,1,0:T(1,128)} %all-to-all-done.1.refs_0_, ...), custom_call_target="tpu_custom_call" | custom-call | tf_op jit(solution)/shard_map/pallas_call | solution.py:359
  48.3 4.9 %all-to-all-start.2 = ((f32[32,1,1536]{2,1,0:T(1,128)}), f32[32,1,1536]{2,1,0:T(1,128)}, u32[]{:S(2)}, u32[]{:S(2)}) async-start(f32[32,1,1536]{2,1,0:T(1,128)} %get-tuple-element.46), calls=%async_computation.2 | async-start | bytes 393216 | tf_op jit(solution)/shard_map/all_to_all | solution.py:405
  53.3 2.7 %collective-permute-start.4 = (f32[3,512]{1,0:T(4,128)}, f32[3,512]{1,0:T(4,128)}, u32[]{:S(2)}, u32[]{:S(2)}) collective-permute-start(f32[3,512]{1,0:T(4,128)} %get-tuple-element.49), channel_id=1, source_target_pairs={{0,4},{4,8},{8,12},{12,16},{16,20},{20,24},{24,28},{1,5},{5,9},{9,... | collective-permute-start | bytes 18440 | tf_op jit(solution)/shard_map/ppermute | solution.py:400
  56.0 1.3 %collective-permute-start.5 = (f32[3,512]{1,0:T(4,128)}, f32[3,512]{1,0:T(4,128)}, u32[]{:S(2)}, u32[]{:S(2)}) collective-permute-start(f32[3,512]{1,0:T(4,128)} %get-tuple-element.50), channel_id=1, source_target_pairs={{4,0},{8,4},{12,8},{16,12},{20,16},{24,20},{28,24},{5,1},{9,5},{13... | collective-permute-start | bytes 18440 | tf_op jit(solution)/shard_map/ppermute | solution.py:401
  57.2 0.0 collective-permute-done.4.refs_18_
  57.3 2.7 %collective-permute-done.5.refs_19_ = f32[3,512]{1,0:T(4,128)} collective-permute-done((f32[3,512]{1,0:T(4,128)}, f32[3,512]{1,0:T(4,128)}, u32[]{:S(2)}, u32[]{:S(2)}) %collective-permute-start.5) | collective-permute-done | bytes 6176 | tf_op jit(solution)/shard_map/ppermute | solution.py:401
  59.9 2.7 %all-to-all-done.2.refs_0_ = f32[32,1,1536]{2,1,0:T(1,128)} async-done(((f32[32,1,1536]{2,1,0:T(1,128)}), f32[32,1,1536]{2,1,0:T(1,128)}, u32[]{:S(2)}, u32[]{:S(2)}) %all-to-all-start.2) | async-done | bytes 196640 | tf_op jit(solution)/shard_map/all_to_all | solution.py:405
  62.6 6.8 %shard_map.243 = (f32[3,32,512]{2,1,0:T(8,128)}, f32[3,32,512]{2,1,0:T(8,128)}, f32[3,32,512]{2,1,0:T(8,128)}, f32[1,384]{1,0:T(1,128)}, f32[32,1,384]{2,1,0:T(1,128)}) custom-call(f32[32,1,1536]{2,1,0:T(1,128)} %all-to-all-done.2.refs_0_, f32[256,256]{1,0:T(8,128)} %shard_map.240.refs_20_.refs_1_, f32[32,1,1920]{2,1,0:T(1,128)} %all-to-all-done.refs_0_.refs_2_, ...), custom_call_target="tpu_custom_call" | custom-call | tf_op jit(solution)/shard_map/pallas_call | solution.py:359
  69.4 12.2 %all_to_all.20.refs_0_ = f32[32,1,384]{2,1,0:T(1,128)} all-to-all(f32[32,1,384]{2,1,0:T(1,128)} %get-tuple-element.54), channel_id=1, replica_groups=mesh['slab'=8,'grp'=4] {'slab','grp'}, dimensions={0} | all-to-all | bytes 98304 | tf_op jit(solution)/shard_map/all_to_all | solution.py:405
  81.6 3.0 %shard_map.244 = (f32[3,32,512]{2,1,0:T(8,128)}, f32[3,32,512]{2,1,0:T(8,128)}) custom-call(f32[32,1,384]{2,1,0:T(1,128)} %all_to_all.20.refs_0_, f32[256,256]{1,0:T(8,128)} %shard_map.240.refs_20_.refs_1_, f32[1,1920]{1,0:T(1,128)} %get-tuple-element.35.refs_18_.refs_22_.refs_2_, bf16[512,256]{1,0:T(8,128)(2,1)} %constant.41.clone.refs_3_.refs_5_.refs_8_, ...), custom_call_target="tpu_custom_call" | custom-call | tf_op jit(solution)/shard_map/pallas_call | solution.py:359
  (1 shorter events, 0.0 us)
Async XLA Ops:
  4.1 17.4 %all-to-all-start = ((f32[32,1,1920]{2,1,0:T(1,128)}), f32[32,1,1920]{2,1,0:T(1,128)}, u32[]{:S(2)}, u32[]{:S(2)}) async-start(f32[32,1,1920]{2,1,0:T(1,128)} %get-tuple-element.30), calls=%async_computation | async-start | bytes 491520 | tf_op jit(solution)/shard_map/all_to_all | solution.py:405
  11.6 6.3 %collective-permute-start = (f32[9,512]{1,0:T(8,128)}, f32[9,512]{1,0:T(8,128)}, u32[]{:S(2)}, u32[]{:S(2)}) collective-permute-start(f32[9,512]{1,0:T(8,128)} %get-tuple-element.33), channel_id=1, source_target_pairs={{0,4},{4,8},{8,12},{12,16},{16,20},{20,24},{24,28},{1,5},{5,9},{9,... | collective-permute-start | bytes 55304 | tf_op jit(solution)/shard_map/ppermute | solution.py:400
  14.2 4.0 %collective-permute-start.1 = (f32[9,512]{1,0:T(8,128)}, f32[9,512]{1,0:T(8,128)}, u32[]{:S(2)}, u32[]{:S(2)}) collective-permute-start(f32[9,512]{1,0:T(8,128)} %get-tuple-element.34), channel_id=1, source_target_pairs={{4,0},{8,4},{12,8},{16,12},{20,16},{24,20},{28,24},{5,1},{9,5},{13... | collective-permute-start | bytes 55304 | tf_op jit(solution)/shard_map/ppermute | solution.py:401
  27.2 13.9 %all-to-all-start.1 = ((f32[32,1,1536]{2,1,0:T(1,128)}), f32[32,1,1536]{2,1,0:T(1,128)}, u32[]{:S(2)}, u32[]{:S(2)}) async-start(f32[32,1,1536]{2,1,0:T(1,128)} %get-tuple-element.37), calls=%async_computation.1 | async-start | bytes 393216 | tf_op jit(solution)/shard_map/all_to_all | solution.py:405
  31.8 4.0 %collective-permute-start.2 = (f32[3,512]{1,0:T(4,128)}, f32[3,512]{1,0:T(4,128)}, u32[]{:S(2)}, u32[]{:S(2)}) collective-permute-start(f32[3,512]{1,0:T(4,128)} %get-tuple-element.40), channel_id=1, source_target_pairs={{0,4},{4,8},{8,12},{12,16},{16,20},{20,24},{24,28},{1,5},{5,9},{9,... | collective-permute-start | bytes 18440 | tf_op jit(solution)/shard_map/ppermute | solution.py:400
  34.4 4.0 %collective-permute-start.3 = (f32[3,512]{1,0:T(4,128)}, f32[3,512]{1,0:T(4,128)}, u32[]{:S(2)}, u32[]{:S(2)}) collective-permute-start(f32[3,512]{1,0:T(4,128)} %get-tuple-element.41), channel_id=1, source_target_pairs={{4,0},{8,4},{12,8},{16,12},{20,16},{24,20},{28,24},{5,1},{9,5},{13... | collective-permute-start | bytes 18440 | tf_op jit(solution)/shard_map/ppermute | solution.py:401
  48.3 14.3 %all-to-all-start.2 = ((f32[32,1,1536]{2,1,0:T(1,128)}), f32[32,1,1536]{2,1,0:T(1,128)}, u32[]{:S(2)}, u32[]{:S(2)}) async-start(f32[32,1,1536]{2,1,0:T(1,128)} %get-tuple-element.46), calls=%async_computation.2 | async-start | bytes 393216 | tf_op jit(solution)/shard_map/all_to_all | solution.py:405
  53.3 4.0 %collective-permute-start.4 = (f32[3,512]{1,0:T(4,128)}, f32[3,512]{1,0:T(4,128)}, u32[]{:S(2)}, u32[]{:S(2)}) collective-permute-start(f32[3,512]{1,0:T(4,128)} %get-tuple-element.49), channel_id=1, source_target_pairs={{0,4},{4,8},{8,12},{12,16},{16,20},{20,24},{24,28},{1,5},{5,9},{9,... | collective-permute-start | bytes 18440 | tf_op jit(solution)/shard_map/ppermute | solution.py:400
  56.0 4.0 %collective-permute-start.5 = (f32[3,512]{1,0:T(4,128)}, f32[3,512]{1,0:T(4,128)}, u32[]{:S(2)}, u32[]{:S(2)}) collective-permute-start(f32[3,512]{1,0:T(4,128)} %get-tuple-element.50), channel_id=1, source_target_pairs={{4,0},{8,4},{12,8},{16,12},{20,16},{24,20},{28,24},{5,1},{9,5},{13... | collective-permute-start | bytes 18440 | tf_op jit(solution)/shard_map/ppermute | solution.py:401
where the time goes:
time: 85.2 us; the launch traced here: 84.6 us
  starting transfers between devices  28.8 us (34%)
  Pallas kernels  28.6 us (34%)
  waiting for transfers between devices  14.3 us (17%)
  blocking collectives  12.2 us (14%)
    pallas_call x6, Pallas kernels, call(): pl.pallas_call(kernel, out_shape=[jax.ShapeDtypeStruct(outs[name], F32) f...  28.6 us
    all_to_all x3, starting transfers between devices, exchange(): return lax.all_to_all(chunk, BOTH, split_axis=0, concat_axis=0, tiled=True)  16.9 us
    all_to_all x1, blocking collectives, exchange(): return lax.all_to_all(chunk, BOTH, split_axis=0, concat_axis=0, tiled=True)  12.2 us
    all_to_all x3, waiting for transfers between devices, exchange(): return lax.all_to_all(chunk, BOTH, split_axis=0, concat_axis=0, tiled=True)  8.66 us
    ppermute x3, starting transfers between devices, neighbours(): lax.ppermute(last, 'slab', [(i, i + 1) for i in range(slabs - 1)])  8.05 us
    ppermute x3, waiting for transfers between devices, neighbours(): lax.ppermute(first, 'slab', [(i + 1, i) for i in range(slabs - 1)])  5.67 us
    ppermute x3, starting transfers between devices, neighbours(): lax.ppermute(first, 'slab', [(i + 1, i) for i in range(slabs - 1)])  3.84 us
  transfers between devices with their start and end apart: 9, of which 6 were waited for; matrix products, arithmetic and copies ran while one was open for 0% of the time, Pallas kernels for 3%

commit v1 on v0

--- a/solution.py
+++ b/solution.py
@@ -62,22 +62,18 @@
     weight = 1.0 / (PRECOND_SHIFT + PRECOND_T * (cross_rows[:, None] + cross_cols[None, :]))
     wave_weight = 1.0 / (PRECOND_SHIFT + PRECOND_T * (cross_waves[:, None] + cross_cols[None, :]))
     first, last = sine_cols[0], sine_cols[-1]
-    answer = np.zeros((2, cols, 128))
+    answer = np.zeros((cols, 128))
     for end, row in enumerate((0, rows - 1)):
         inside = PRECOND_T * np.einsum("ri,ij,i->jr", sine_rows, weight, sine_rows[:, row])
-        answer[end, :, :rows] = first[:, None] * inside
-        answer[end, :, rows : 2 * rows] = last[:, None] * inside
+        answer[:, 64 * end : 64 * end + rows] = first[:, None] * inside
+        answer[:, 64 * end + rows : 64 * end + 2 * rows] = last[:, None] * inside
     spread_rows = np.repeat(np.eye(rows // 8), 8, axis=0)
     spread_cols = np.repeat(np.eye(cols // 8), 8, axis=0)
     mode_rows, mode_cols = sine_rows @ spread_rows, sine_cols @ spread_cols
     mixed = np.einsum("ri,ij,ib->rbj", sine_rows, weight, mode_rows)
-    coarse = np.zeros((rows // 8, cols // 8, 2 * cols + 128))
-    coarse[:, :, :cols] = np.einsum("bj,jc->bcj", mixed[0], mode_cols)
-    coarse[:, :, cols : 2 * cols] = np.einsum("bj,jc->bcj", mixed[-1], mode_cols)
-    coarse[:, :, 2 * cols : 2 * cols + rows] = np.einsum("rbj,j,jc->bcr", mixed, first, mode_cols)
-    coarse[:, :, 2 * cols + rows : 2 * cols + 2 * rows] = np.einsum(
-        "rbj,j,jc->bcr", mixed, last, mode_cols
-    )
+    coarse = np.zeros((rows // 8, cols // 8, 128))
+    coarse[:, :, :rows] = np.einsum("rbj,j,jc->bcr", mixed, first, mode_cols)
+    coarse[:, :, rows : 2 * rows] = np.einsum("rbj,j,jc->bcr", mixed, last, mode_cols)
     column_chain = chain_tables(cross_waves, cols_total, cols)
     tile = max(8, groups)
     own_columns = np.zeros((groups, 4, tile, rows_total))
@@ -98,22 +94,23 @@
         own_columns=own_columns.reshape(groups, 4 * tile, rows_total),
         around=around,
         ends=ends,
-        place=np.tile(np.eye(cols // 8), (1, rows // 8)),
+        coarse_rows=np.concatenate([mixed[0], mixed[-1]]),
     )
     split = dict(
         sine_rows=sine_rows,
         sine_cols=sine_cols,
-        answer=answer.reshape(2 * cols, 128),
-        coarse=coarse.reshape(blocks, 2 * cols + 128),
+        answer=answer,
+        coarse=coarse.reshape(blocks, 128),
         waves=waves,
         wave_weight=wave_weight,
-        up_modes=down.T @ sine_cols,
+        up_modes=np.tile(mode_cols.T, (128 // (cols // 8), 1)),
     )
     tables = {name: np.asarray(table, np.float32) for name, table in exact.items()}
     for name, table in split.items():
         high = table.astype(jnp.bfloat16)
         tables[name] = np.stack([high, (table - high.astype(np.float64)).astype(jnp.bfloat16)])
     tables["down"] = down.astype(jnp.bfloat16)
+    tables["place"] = np.tile(np.eye(cols // 8), (1, rows // 8)).astype(jnp.bfloat16)
     return tables
 
 
@@ -214,23 +211,21 @@
     return jnp.sum(jnp.where(own, spread, 0.0), axis=0, keepdims=True)
 
 
-def zone_totals(surface, zone_line, down, zones):
+def zone_totals(surface, hot, down):
     rows, cols = surface.shape
     sums = [jnp.sum(surface[8 * i : 8 * i + 8], axis=0, keepdims=True) for i in range(rows // 8)]
     sums = jnp.concatenate(sums + [jnp.zeros((8 - rows // 8, cols), F32)], axis=0)
     line = to_line(mm_exact(sums, down), cols // 8)
-    blocks = zone_line.shape[1]
-    hot = (iota((zones, blocks), 0) == zone_line.astype(jnp.int32)).astype(F32).astype(BF16)
-    line = jnp.broadcast_to(line, (8, blocks))
+    line = jnp.broadcast_to(line, (8, line.shape[1]))
     return mm_exact(line, hot, DIMS_T)[0:1]
 
 
-def field_rows(lines, down, block_rows, block_cols):
+def field_rows(lines, down, block_cols):
     row, place = iota((8, lines[0][0].shape[1]), 0), iota((8, lines[0][0].shape[1]), 1) // block_cols
     picked = jnp.zeros(row.shape, F32)
     for index, (line, wanted) in enumerate(lines):
         picked = jnp.where((row == index) & (place == wanted), line, picked)
-    return mm_exact(picked, down, DIMS_T), picked
+    return mm_exact(picked, down, DIMS_T)
 
 
 def spread_rows8(lines, rows):
@@ -256,7 +251,9 @@
     own_before = jnp.sum(jnp.where(mine, before, 0.0), axis=0, keepdims=True)
     own_after = jnp.sum(jnp.where(mine, after, 0.0), axis=0, keepdims=True)
     answer = t.answer
-    edges = edges + mm(jnp.concatenate([before, after], axis=1), answer)
+    moved = mm(jnp.concatenate([before, after], axis=0), answer)
+    lane = iota(edges.shape, 1)
+    edges = edges + jnp.where(lane < 64, moved[:devices] + pltpu.roll(moved[devices:], 64, 1), 0.0)
     tile, per = max(8, groups), 128 // rows
     lane = iota(edges.shape, 1) // rows
     lines = []
@@ -355,14 +352,15 @@
         for copy in sent:
             copy.wait()
 
+    kinds = [value if isinstance(value[-1], type(F32)) else (value, F32) for value in outs.values()]
     buffers = [pltpu.VMEM(shape_of(*pairs[place]), arrays[place].dtype) for place in copied]
     made = pl.pallas_call(
         kernel,
-        out_shape=[jax.ShapeDtypeStruct(outs[name], F32) for name in results],
+        out_shape=[jax.ShapeDtypeStruct(*kind) for kind in kinds],
         in_specs=[pl.BlockSpec(memory_space=pl.ANY)] * len(names),
         out_specs=[pl.BlockSpec(memory_space=pl.ANY)] * len(results),
         scratch_shapes=buffers
-        + [pltpu.VMEM(outs[name], F32) for name in results]
+        + [pltpu.VMEM(*kind) for kind in kinds]
         + [pltpu.SemaphoreType.DMA((len(copied),)), pltpu.SemaphoreType.DMA((len(results),))],
         compiler_params=pltpu.CompilerParams(vmem_limit_bytes=VMEM_LIMIT),
     )(*arrays)
@@ -395,11 +393,16 @@
     widths = (at_sides + 5 * 128, at_zones + zones + 2 * 128)
     area = (layers, rows, cols)
 
-    def neighbours(first, last):
+    def neighbours(near, far):
+        across = [(i, i + 1) for i in range(1, slabs - 1, 2)]
         return (
-            lax.ppermute(last, "slab", [(i, i + 1) for i in range(slabs - 1)]),
-            lax.ppermute(first, "slab", [(i + 1, i) for i in range(slabs - 1)]),
+            lax.ppermute(near, "slab", [(i, i ^ 1) for i in range(slabs)]),
+            lax.ppermute(far, "slab", across + [(j, i) for i, j in across]),
         )
+
+    def choose(near, far):
+        odd = lax.axis_index("slab") % 2 == 1
+        return jnp.where(odd, near, far), jnp.where(odd, far, near)
 
     def exchange(chunk):
         return lax.all_to_all(chunk, BOTH, split_axis=0, concat_axis=0, tiled=True)
@@ -407,10 +410,10 @@
     def start_body(get, out, done):
         ids = get.zone_of_block[...].astype(F32)
         ids = jnp.concatenate([ids, jnp.zeros((8 - block_rows, block_cols), F32)], axis=0)
-        zone_line = to_line(mm_f32(ids, get.place[...]), block_cols)
+        zone_line = to_line(mm_exact(ids, get.place[...]), block_cols)
         index = jnp.broadcast_to(zone_line, (8, blocks)).astype(jnp.int32)
         found = lookup(get.zone_recharge[...], index)[0:1]
-        field, _ = field_rows([(found, i) for i in range(block_rows)], get.down[...], block_rows, block_cols)
+        field = field_rows([(found, i) for i in range(block_rows)], get.down[...], block_cols)
         source_ref, rhs = get.source, out.rhs
         rhs[0] = source_ref[0] + spread_rows8(field, rows)
         for layer in range(1, layers):
@@ -423,7 +426,7 @@
         out.q_mixed[...] = q_mixed
         done(out.q_mixed)
         cond, store, leak = get.conductivity, get.storage, get.leakance
-        partial, halo = out.partial, (out.first, out.last)
+        partial, edge_rows = out.partial, [[], []]
         for layer in range(layers):
             own = cond[layer]
             diagonal = store[layer] + 0.5 * (4.0 * own + stencil(own, 0.0, 0.0, 0.0, 0.0))
@@ -435,10 +438,13 @@
                 diagonal = diagonal + get.et_rate[...]
             partial[layer] = diagonal
             for end, row in enumerate((0, rows - 1)):
-                halo[end][layer : layer + 1] = own[row : row + 1]
-                halo[end][layers + layer : layers + layer + 1] = diagonal[row : row + 1]
-                halo[end][2 * layers + layer : 2 * layers + layer + 1] = rhs[layer, row : row + 1]
-        done(out.partial, out.first, out.last)
+                edge_rows[end] += [own[row : row + 1], diagonal[row : row + 1], rhs[layer, row : row + 1]]
+        first, last = [
+            jnp.concatenate([rows_of[place] for kind in range(3) for place in range(kind, 3 * layers, 3)], axis=0)
+            for rows_of in edge_rows
+        ]
+        out.near[...], out.far[...] = choose(first, last)
+        done(out.partial, out.near, out.far)
         first, last, left, right = rings(q_mixed, get)
         line, chunk = out.line, out.chunk
         line[:, :cols] = first
@@ -478,16 +484,15 @@
             rhs=area,
             q_mixed=(rows, cols),
             partial=area,
-            first=(3 * layers, cols),
-            last=(3 * layers, cols),
+            near=(3 * layers, cols),
+            far=(3 * layers, cols),
             line=(1, widths[0]),
             chunk=(devices, 1, widths[0]),
         ),
     )
     rhs = started.rhs
     received = first_received = exchange(started.chunk)
-    halo_north, halo_south = neighbours(started.first, started.last)
-    first_north, first_south = halo_north, halo_south
+    near, far = first_near, first_far = neighbours(started.near, started.far)
 
     def couple_body(get, out, done):
         ids, weights = get.pair_zones, get.pair_weight
@@ -497,13 +502,17 @@
         own = iota((zones, zones), 0) == iota((zones, zones), 1)
         matrix = matrix + jnp.where(own, get.zone_weight[...], 0.0)
         out.couple[...] = (COUPLE * zones / (slabs * rows * groups * cols)) * matrix
-        done(out.couple)
-
-    couple = call(
+        line = get.line[:, at_zones:at_sides].astype(jnp.int32)
+        out.hot[...] = (iota((zones, blocks), 0) == line).astype(F32).astype(BF16)
+        done(out.couple, out.hot)
+
+    coupling = call(
         couple_body,
-        dict(pair_zones=pair_zones.T, pair_weight=pair_weight[None], zone_weight=zone_weight[None]),
-        dict(couple=(zones, zones)),
-    ).couple
+        dict(pair_zones=pair_zones.T, pair_weight=pair_weight[None], zone_weight=zone_weight[None])
+        | dict(line=started.line),
+        dict(couple=(zones, zones), hot=((zones, blocks), BF16)),
+    )
+    couple, hot = coupling.couple, coupling.hot
 
     def step_body(number, get, out, done):
         coupled, final = number > 0, number == 2
@@ -534,10 +543,22 @@
             totals = jnp.sum(recv[:, 0, at_zones : at_zones + zones], axis=0, keepdims=True)
             reply = mm_f32(jnp.broadcast_to(totals, (8, zones)), get.couple[...])[0:1]
             every = lookup(reply, get.zone_map[:, 0, :].astype(jnp.int32))
-            coarse = mm(every, get.coarse)
-            first_rows = first_rows + coarse[:, :cols]
-            last_rows = last_rows + coarse[:, cols : 2 * cols]
-            edges = edges + coarse[:, 2 * cols :]
+            edges = edges + mm(every, get.coarse)
+            share = 128 // block_cols
+            inner = iota((devices, 128), 1) // block_cols
+            slabs_of = [
+                jnp.where(inner == i % share, every[:, 128 * (i // share) : 128 * (i // share + 1)], 0.0)
+                for i in range(block_rows)
+            ]
+            modes_of = mm(jnp.concatenate(slabs_of, axis=0), get.up_modes)
+            device = iota(first_rows.shape, 0)
+            modes = []
+            for i in range(block_rows):
+                part = modes_of[devices * i : devices * (i + 1)]
+                first_rows = first_rows + get.coarse_rows[i : i + 1] * part
+                last_rows = last_rows + get.coarse_rows[block_rows + i : block_rows + i + 1] * part
+                modes.append(jnp.sum(jnp.where(device == own, part, 0.0), axis=0, keepdims=True))
+            modes = jnp.concatenate(modes, axis=0)
             device = iota(every.shape, 0)
             line_of = lambda shift: jnp.sum(
                 jnp.where(device == own + shift, every, 0.0), axis=0, keepdims=True
@@ -545,8 +566,7 @@
             mine = line_of(0)
             wanted = [(mine, i) for i in range(block_rows)]
             wanted += [(line_of(-groups), block_rows - 1), (line_of(groups), 0)]
-            field, picked = field_rows(wanted, get.down[...], block_rows, block_cols)
-            modes = mm(picked, get.up_modes)
+            field = field_rows(wanted, get.down[...], block_cols)
             q_in = q_in + spread_rows8(modes, rows)
             surface = surface + spread_rows8(field, rows)
             column = iota((rows, blocks), 1)
@@ -569,10 +589,10 @@
             first_rows, last_rows, edges, q_in, slab, group, groups, get
         )
         cond, leak = get.conductivity, get.leakance
-        north_ref, south_ref = get.north, get.south
+        north_ref, south_ref = choose(get.near[...], get.far[...])
         row, col = iota((rows, cols), 0), iota((rows, cols), 1)
         if coupled:
-            cond_north, cond_south = get.first_north, get.first_south
+            cond_north, cond_south = choose(get.first_near[...], get.first_far[...])
             sides = get.sides
             lanes = [of(-1, sides_at + 128), of(1, sides_at)]
             diagonal_ref, inverse_ref = get.diagonal, get.inverse
@@ -686,7 +706,7 @@
             images.append(image)
         done(out.image)
         line, chunk = out.line, out.chunk
-        totals = zone_totals(fields[0], get.zone_line[:, at_zones:at_sides], get.down[...], zones)
+        totals = zone_totals(fields[0], get.hot[...], get.down[...])
         if final:
             rhs_ref, v0_ref, v1_ref, w0_ref = get.rhs, get.v0, get.v1, get.w0
 
@@ -714,10 +734,11 @@
             out.q_mixed[...] = q_next
             done(out.q_mixed)
             scaled = [images[layer] * inverse_ref[layer] for layer in range(layers)]
-            for layer in range(layers):
-                out.first[layer : layer + 1] = scaled[layer][0:1]
-                out.last[layer : layer + 1] = scaled[layer][rows - 1 : rows]
-            done(out.first, out.last)
+            out.near[...], out.far[...] = choose(
+                jnp.concatenate([part[0:1] for part in scaled], axis=0),
+                jnp.concatenate([part[rows - 1 : rows] for part in scaled], axis=0),
+            )
+            done(out.near, out.far)
             first, last, left, right = rings(q_next, get)
             west, east = side_lanes(scaled, (left, right))
             line[:, :cols] = first
@@ -731,20 +752,18 @@
     tail_width = zones + 128
     shared = {}
 
-    def step(number, received, q_mixed, w, north, south, more=()):
+    def step(number, received, q_mixed, w, near, far, more=()):
         ins = dict(received=received)
         if number > 0:
-            ins |= dict(couple=couple, zone_map=zone_map, coarse=t.coarse)
+            ins |= dict(couple=couple, zone_map=zone_map, coarse=t.coarse, up_modes=t.up_modes, coarse_rows=t.coarse_rows)
         ins |= dict(row_chain=t.row_chain, answer=t.answer, q_mixed=q_mixed, w=w, down=t.down)
-        if number > 0:
-            ins |= dict(up_modes=t.up_modes)
         ins |= dict(waves=t.waves, own_columns=t.own_columns, around=t.around, wave_weight=t.wave_weight)
         ins |= dict(ends=t.ends, sine_rows=t.sine_rows, weight=t.weight, sine_cols=t.sine_cols)
-        ins |= dict(north=north, south=south, conductivity=conductivity, leakance=leakance)
-        ins |= dict(zone_line=started.line)
+        ins |= dict(near=near, far=far, conductivity=conductivity, leakance=leakance)
+        ins |= dict(hot=hot)
         outs = dict(v=area, image=area)
         if number > 0:
-            ins |= dict(first_north=first_north, first_south=first_south) | shared
+            ins |= dict(first_near=first_near, first_far=first_far) | shared
             outs |= dict(w=area)
         else:
             ins |= dict(partial=started.partial, couple=(couple, None))
@@ -754,20 +773,20 @@
             outs |= dict(line=(1, tail_width), chunk=(devices, 1, tail_width))
         else:
             outs |= dict(
-                q_mixed=(rows, cols), first=(layers, cols), last=(layers, cols), line=(1, widths[1]), chunk=(devices, 1, widths[1])
+                q_mixed=(rows, cols), near=(layers, cols), far=(layers, cols), line=(1, widths[1]), chunk=(devices, 1, widths[1])
             )
         return call(lambda get, out, done: step_body(number, get, out, done), ins, outs)
 
-    one = step(0, received, started.q_mixed, rhs, halo_north, halo_south)
+    one = step(0, received, started.q_mixed, rhs, near, far)
     shared.update(diagonal=one.diagonal, inverse=one.inverse, sides=one.sides, beside=one.beside)
     zone_map = (first_received, (slice(None), slice(None), slice(at_zones, at_sides)))
     received = exchange(one.chunk)
-    halo_north, halo_south = neighbours(one.first, one.last)
-    two = step(1, received, one.q_mixed, one.image, halo_north, halo_south)
+    near, far = neighbours(one.near, one.far)
+    two = step(1, received, one.q_mixed, one.image, near, far)
     received = exchange(two.chunk)
-    halo_north, halo_south = neighbours(two.first, two.last)
+    near, far = neighbours(two.near, two.far)
     more = dict(rhs=rhs, v0=one.v, v1=two.v, w0=two.w)
-    three = step(2, received, two.q_mixed, two.image, halo_north, halo_south, more)
+    three = step(2, received, two.q_mixed, two.image, near, far, more)
     received = exchange(three.chunk)
 
     def finish_body(get, out, done):
@@ -777,7 +796,7 @@
         zone_line = get.zone_line[:, at_zones:at_sides]
         index = jnp.broadcast_to(zone_line, (8, blocks)).astype(jnp.int32)
         found = lookup(reply[0:1], index)[0:1]
-        field, _ = field_rows([(found, i) for i in range(block_rows)], get.down[...], block_rows, block_cols)
+        field = field_rows([(found, i) for i in range(block_rows)], get.down[...], block_cols)
         coupled = spread_rows8(field, rows)
         a00, a01, a11, a02, a12, a22, h0, h1, h2 = [sums[:, zones + i : zones + i + 1] for i in range(9)]
         a22 = a22 + jnp.sum(totals * reply[0:1], axis=1, keepdims=True)

time: 85.2 us -> 79.9 us (0.938)
  starting transfers between devices: 28.8 us -> 18.2 us
  waiting for transfers between devices: 14.3 us -> 22 us
  blocking collectives: 12.2 us -> 10.5 us
    all_to_all x3, waiting for transfers between devices: 8.66 us -> 21.9 us  [exchange(): return lax.all_to_all(chunk, BOTH, split_axis=0, concat_axis=0, tiled=True)]
    ppermute x6, starting transfers between devices: 11.9 us -> 4.22 us  [the longest x3 3.75 us: neighbours(): lax.ppermute(far, 'slab', across + [(j, i) for i, j in across])]
    ppermute x6, waiting for transfers between devices: 5.68 us -> 0.03 us  [the longest x3 0.02 us: neighbours(): lax.ppermute(near, 'slab', [(i, i ^ 1) for i in range(slabs)])]
    all_to_all x3, starting transfers between devices: 16.9 us -> 14 us  [exchange(): return lax.all_to_all(chunk, BOTH, split_axis=0, concat_axis=0, tiled=True)]
    all_to_all x1, blocking collectives: 12.2 us -> 10.5 us  [exchange(): return lax.all_to_all(chunk, BOTH, split_axis=0, concat_axis=0, tiled=True)]
  transfers between devices with their start and end apart: 9 -> 9, of which waited for: 6 -> 3; matrix products, arithmetic and copies ran while one was open for 0% -> 0% of each run, Pallas kernels for 3% -> 3%
where the time goes in v1:
time: 79.9 us; the launch traced here: 79.3 us
  Pallas kernels  27.8 us (35%)
  waiting for transfers between devices  22 us (28%)
  starting transfers between devices  18.2 us (23%)
  blocking collectives  10.5 us (13%)
    pallas_call x6, Pallas kernels, call(): pl.pallas_call(kernel, out_shape=[jax.ShapeDtypeStruct(*kind) for kind in...  27.8 us
    all_to_all x3, waiting for transfers between devices, exchange(): return lax.all_to_all(chunk, BOTH, split_axis=0, concat_axis=0, tiled=True)  21.9 us
    all_to_all x3, starting transfers between devices, exchange(): return lax.all_to_all(chunk, BOTH, split_axis=0, concat_axis=0, tiled=True)  14 us
    all_to_all x1, blocking collectives, exchange(): return lax.all_to_all(chunk, BOTH, split_axis=0, concat_axis=0, tiled=True)  10.5 us
    ppermute x3, starting transfers between devices, neighbours(): lax.ppermute(far, 'slab', across + [(j, i) for i, j in across])  3.75 us
  transfers between devices with their start and end apart: 9, of which 3 were waited for; matrix products, arithmetic and copies ran while one was open for 0% of the time, Pallas kernels for 3%

profile of v1, /device:TPU:0, one launch (start us, length us, event | category | flops | bytes accessed | tf_op | source)
XLA Modules:
  0.0 79.3 jit_solution(15020981134674260778)
XLA Ops:
  0.6 3.4 %shard_map.248 = (f32[3,32,512]{2,1,0:T(8,128)}, f32[32,512]{1,0:T(8,128)}, f32[3,32,512]{2,1,0:T(8,128)}, f32[9,512]{1,0:T(8,128)}, f32[9,512]{1,0:T(8,128)}, /...) custom-call(s32[4,64]{1,0:T(4,128)} %refs_0_.1, f32[1,256]{1,0:T(1,128)} %bitcast.6, bf16[64,256]{1,0:T(8,128)(2,1)} %constant.44.clone.refs_2_, ...), custom_call_target="tpu_custom_call" | custom-call | tf_op jit(solution)/shard_map/pallas_call | solution.py:357
  4.1 7.4 %all-to-all-start = ((f32[32,1,1920]{2,1,0:T(1,128)}), f32[32,1,1920]{2,1,0:T(1,128)}, u32[]{:S(2)}, u32[]{:S(2)}) async-start(f32[32,1,1920]{2,1,0:T(1,128)} %get-tuple-element.32), calls=%async_computation | async-start | bytes 491520 | tf_op jit(solution)/shard_map/all_to_all | solution.py:408
  11.5 0.3 collective-permute-start
  11.8 1.3 %collective-permute-start.1 = (f32[9,512]{1,0:T(8,128)}, f32[9,512]{1,0:T(8,128)}, u32[]{:S(2)}, u32[]{:S(2)}) collective-permute-start(f32[9,512]{1,0:T(8,128)} %get-tuple-element.36), channel_id=1, source_target_pairs={{4,8},{12,16},{20,24},{8,4},{16,12},{24,20},{5,9},{13,17},{21,25},... | collective-permute-start | bytes 55304 | tf_op jit(solution)/shard_map/ppermute | solution.py:400
  13.0 2.4 %shard_map.249 = (f32[256,256]{1,0:T(8,128)}, bf16[256,256]{1,0:T(8,128)(2,1)}) custom-call(s32[2,512]{1,0:T(2,128)} %bitcast.4, f32[1,512]{1,0:T(1,128)} %bitcast.5, f32[1,256]{1,0:T(1,128)} %bitcast.7, f32[1,1920]{1,0:T(1,128)} %get-tuple-element.37.refs_3_.refs_2_), custom_call_target="tpu_custom_call" | custom-call | tf_op jit(solution)/shard_map/pallas_call | solution.py:357
  15.4 0.0 collective-permute-done.refs_14_.refs_24_
  15.4 0.0 collective-permute-done.1.refs_15_.refs_25_
  15.4 6.1 %all-to-all-done.refs_0_.refs_2_ = f32[32,1,1920]{2,1,0:T(1,128)} async-done(((f32[32,1,1920]{2,1,0:T(1,128)}), f32[32,1,1920]{2,1,0:T(1,128)}, u32[]{:S(2)}, u32[]{:S(2)}) %all-to-all-start) | async-done | bytes 245792 | tf_op jit(solution)/shard_map/all_to_all | solution.py:408
  21.5 5.6 %shard_map.250 = (f32[3,32,512]{2,1,0:T(8,128)}, f32[3,32,512]{2,1,0:T(8,128)}, f32[3,32,512]{2,1,0:T(8,128)}, f32[3,32,512]{2,1,0:T(8,128)}, f32[4,32,128]{2,1,...) custom-call(f32[32,1,1920]{2,1,0:T(1,128)} %all-to-all-done.refs_0_., ...), custom_call_target="tpu_custom_call" | custom-call | tf_op jit(solution)/shard_map/pallas_call | solution.py:357
  27.2 3.3 %all-to-all-start.1 = ((f32[32,1,1536]{2,1,0:T(1,128)}), f32[32,1,1536]{2,1,0:T(1,128)}, u32[]{:S(2)}, u32[]{:S(2)}) async-start(f32[32,1,1536]{2,1,0:T(1,128)} %get-tuple-element.41), calls=%async_computation.1 | async-start | bytes 393216 | tf_op jit(solution)/shard_map/all_to_all | solution.py:408
  30.5 0.1 collective-permute-start.2
  30.6 1.2 %collective-permute-start.3 = (f32[3,512]{1,0:T(4,128)S(1)}, f32[3,512]{1,0:T(4,128)}, u32[]{:S(2)}, u32[]{:S(2)}) collective-permute-start(f32[3,512]{1,0:T(4,128)S(1)} %copy-done), channel_id=1, source_target_pairs={{4,8},{12,16},{20,24},{8,4},{16,12},{24,20},{5,9},{13,17},{21,25},... | collective-permute-start | bytes 18440 | tf_op jit(solution)/shard_map/ppermute | solution.py:400
  31.8 0.0 collective-permute-done.2.refs_19_
  31.8 0.0 collective-permute-done.3.refs_20_
  31.8 7.9 %all-to-all-done.1.refs_0_ = f32[32,1,1536]{2,1,0:T(1,128)} async-done(((f32[32,1,1536]{2,1,0:T(1,128)}), f32[32,1,1536]{2,1,0:T(1,128)}, u32[]{:S(2)}, u32[]{:S(2)}) %all-to-all-start.1) | async-done | bytes 196640 | tf_op jit(solution)/shard_map/all_to_all | solution.py:408
  39.8 6.9 %shard_map.251 = (f32[3,32,512]{2,1,0:T(8,128)}, f32[3,32,512]{2,1,0:T(8,128)}, f32[3,32,512]{2,1,0:T(8,128)}, f32[32,512]{1,0:T(8,128)}, f32[3,512]{1,0:T(4,128...) custom-call(f32[32,1,1536]{2,1,0:T(1,128)} %all-to-all-done.1.refs_0_, ...), custom_call_target="tpu_custom_call" | custom-call | tf_op jit(solution)/shard_map/pallas_call | solution.py:357
  46.7 3.3 %all-to-all-start.2 = ((f32[32,1,1536]{2,1,0:T(1,128)}), f32[32,1,1536]{2,1,0:T(1,128)}, u32[]{:S(2)}, u32[]{:S(2)}) async-start(f32[32,1,1536]{2,1,0:T(1,128)} %get-tuple-element.50), calls=%async_computation.2 | async-start | bytes 393216 | tf_op jit(solution)/shard_map/all_to_all | solution.py:408
  50.0 0.1 collective-permute-start.4
  50.1 1.2 %collective-permute-start.5 = (f32[3,512]{1,0:T(4,128)S(1)}, f32[3,512]{1,0:T(4,128)}, u32[]{:S(2)}, u32[]{:S(2)}) collective-permute-start(f32[3,512]{1,0:T(4,128)S(1)} %copy-done.1), channel_id=1, source_target_pairs={{4,8},{12,16},{20,24},{8,4},{16,12},{24,20},{5,9},{13,17},{21,25},... | collective-permute-start | bytes 18440 | tf_op jit(solution)/shard_map/ppermute | solution.py:400
  51.4 0.0 collective-permute-done.4.refs_19_
  51.4 7.9 %all-to-all-done.2.refs_0_ = f32[32,1,1536]{2,1,0:T(1,128)} async-done(((f32[32,1,1536]{2,1,0:T(1,128)}), f32[32,1,1536]{2,1,0:T(1,128)}, u32[]{:S(2)}, u32[]{:S(2)}) %all-to-all-start.2) | async-done | bytes 196640 | tf_op jit(solution)/shard_map/all_to_all | solution.py:408
  59.3 6.5 %shard_map.252 = (f32[3,32,512]{2,1,0:T(8,128)}, f32[3,32,512]{2,1,0:T(8,128)}, f32[3,32,512]{2,1,0:T(8,128)}, f32[1,384]{1,0:T(1,128)}, f32[32,1,384]{2,1,0:T(1,128)}) custom-call(f32[32,1,1536]{2,1,0:T(1,128)} %all-to-all-done.2.refs_0_, f32[256,256]{1,0:T(8,128)} %get-tuple-element.40.refs_20_.refs_1_, f32[32,1,1920]{2,1,0:T(1,128)} %all-to-all-done.refs_0_.refs_2_, ...), custom_call_target="tpu_custom_call" | custom-call | tf_op jit(solution)/shard_map/pallas_call | solution.py:357
  65.8 10.5 %all_to_all.20.refs_0_ = f32[32,1,384]{2,1,0:T(1,128)} all-to-all(f32[32,1,384]{2,1,0:T(1,128)} %get-tuple-element.58), channel_id=1, replica_groups=mesh['slab'=8,'grp'=4] {'slab','grp'}, dimensions={0} | all-to-all | bytes 98304 | tf_op jit(solution)/shard_map/all_to_all | solution.py:408
  76.3 3.0 %shard_map.253 = (f32[3,32,512]{2,1,0:T(8,128)}, f32[3,32,512]{2,1,0:T(8,128)}) custom-call(f32[32,1,384]{2,1,0:T(1,128)} %all_to_all.20.refs_0_, f32[256,256]{1,0:T(8,128)} %get-tuple-element.40.refs_20_.refs_1_, f32[1,1920]{1,0:T(1,128)} %get-tuple-element.37.refs_3_.refs_2_, bf16[512,256]{1,0:T(8,128)(2,1)} %constant.43.clone.refs_3_.refs_5_.refs_10_, ...), custom_call_target="tpu_custom_call" | custom-call | tf_op jit(solution)/shard_map/pallas_call | solution.py:357
  (9 shorter events, 0.0 us)
Async XLA Ops:
  4.1 17.4 %all-to-all-start = ((f32[32,1,1920]{2,1,0:T(1,128)}), f32[32,1,1920]{2,1,0:T(1,128)}, u32[]{:S(2)}, u32[]{:S(2)}) async-start(f32[32,1,1920]{2,1,0:T(1,128)} %get-tuple-element.32), calls=%async_computation | async-start | bytes 491520 | tf_op jit(solution)/shard_map/all_to_all | solution.py:408
  11.5 3.9 %collective-permute-start = (f32[9,512]{1,0:T(8,128)}, f32[9,512]{1,0:T(8,128)}, u32[]{:S(2)}, u32[]{:S(2)}) collective-permute-start(f32[9,512]{1,0:T(8,128)} %get-tuple-element.35), channel_id=1, source_target_pairs={{0,4},{4,0},{8,12},{12,8},{16,20},{20,16},{24,28},{28,24},{1,5},{5... | collective-permute-start | bytes 55304 | tf_op jit(solution)/shard_map/ppermute | solution.py:399
  11.8 3.7 %collective-permute-start.1 = (f32[9,512]{1,0:T(8,128)}, f32[9,512]{1,0:T(8,128)}, u32[]{:S(2)}, u32[]{:S(2)}) collective-permute-start(f32[9,512]{1,0:T(8,128)} %get-tuple-element.36), channel_id=1, source_target_pairs={{4,8},{12,16},{20,24},{8,4},{16,12},{24,20},{5,9},{13,17},{21,25},... | collective-permute-start | bytes 55304 | tf_op jit(solution)/shard_map/ppermute | solution.py:400
  27.1 3.3 %copy-start.2 = (f32[3,512]{1,0:T(4,128)S(1)}, f32[3,512]{1,0:T(4,128)}, u32[]{:S(2)}) copy-start(f32[3,512]{1,0:T(4,128)} %get-tuple-element.44) | copy-start | bytes 18436
  27.1 3.4 %copy-start = (f32[3,512]{1,0:T(4,128)S(1)}, f32[3,512]{1,0:T(4,128)}, u32[]{:S(2)}) copy-start(f32[3,512]{1,0:T(4,128)} %get-tuple-element.45) | copy-start | bytes 18436
  27.2 12.6 %all-to-all-start.1 = ((f32[32,1,1536]{2,1,0:T(1,128)}), f32[32,1,1536]{2,1,0:T(1,128)}, u32[]{:S(2)}, u32[]{:S(2)}) async-start(f32[32,1,1536]{2,1,0:T(1,128)} %get-tuple-element.41), calls=%async_computation.1 | async-start | bytes 393216 | tf_op jit(solution)/shard_map/all_to_all | solution.py:408
  30.5 1.4 %collective-permute-start.2 = (f32[3,512]{1,0:T(4,128)S(1)}, f32[3,512]{1,0:T(4,128)}, u32[]{:S(2)}, u32[]{:S(2)}) collective-permute-start(f32[3,512]{1,0:T(4,128)S(1)} %copy-done.2), channel_id=1, source_target_pairs={{0,4},{4,0},{8,12},{12,8},{16,20},{20,16},{24,28},{28,24},{1,5},{5... | collective-permute-start | bytes 18440 | tf_op jit(solution)/shard_map/ppermute | solution.py:399
  30.6 1.3 %collective-permute-start.3 = (f32[3,512]{1,0:T(4,128)S(1)}, f32[3,512]{1,0:T(4,128)}, u32[]{:S(2)}, u32[]{:S(2)}) collective-permute-start(f32[3,512]{1,0:T(4,128)S(1)} %copy-done), channel_id=1, source_target_pairs={{4,8},{12,16},{20,24},{8,4},{16,12},{24,20},{5,9},{13,17},{21,25},... | collective-permute-start | bytes 18440 | tf_op jit(solution)/shard_map/ppermute | solution.py:400
  46.7 3.3 %copy-start.3 = (f32[3,512]{1,0:T(4,128)S(1)}, f32[3,512]{1,0:T(4,128)}, u32[]{:S(2)}) copy-start(f32[3,512]{1,0:T(4,128)} %get-tuple-element.53) | copy-start | bytes 18436
  46.7 3.5 %copy-start.1 = (f32[3,512]{1,0:T(4,128)S(1)}, f32[3,512]{1,0:T(4,128)}, u32[]{:S(2)}) copy-start(f32[3,512]{1,0:T(4,128)} %get-tuple-element.54) | copy-start | bytes 18436
  46.7 12.6 %all-to-all-start.2 = ((f32[32,1,1536]{2,1,0:T(1,128)}), f32[32,1,1536]{2,1,0:T(1,128)}, u32[]{:S(2)}, u32[]{:S(2)}) async-start(f32[32,1,1536]{2,1,0:T(1,128)} %get-tuple-element.50), calls=%async_computation.2 | async-start | bytes 393216 | tf_op jit(solution)/shard_map/all_to_all | solution.py:408
  50.0 1.4 %collective-permute-start.4 = (f32[3,512]{1,0:T(4,128)S(1)}, f32[3,512]{1,0:T(4,128)}, u32[]{:S(2)}, u32[]{:S(2)}) collective-permute-start(f32[3,512]{1,0:T(4,128)S(1)} %copy-done.3), channel_id=1, source_target_pairs={{0,4},{4,0},{8,12},{12,8},{16,20},{20,16},{24,28},{28,24},{1,5},{5... | collective-permute-start | bytes 18440 | tf_op jit(solution)/shard_map/ppermute | solution.py:399
  50.1 1.3 %collective-permute-start.5 = (f32[3,512]{1,0:T(4,128)S(1)}, f32[3,512]{1,0:T(4,128)}, u32[]{:S(2)}, u32[]{:S(2)}) collective-permute-start(f32[3,512]{1,0:T(4,128)S(1)} %copy-done.1), channel_id=1, source_target_pairs={{4,8},{12,16},{20,24},{8,4},{16,12},{24,20},{5,9},{13,17},{21,25},... | collective-permute-start | bytes 18440 | tf_op jit(solution)/shard_map/ppermute | solution.py:400

commit v2 on v1

--- a/solution.py
+++ b/solution.py
@@ -14,7 +14,7 @@
 PRECOND_SHIFT = 3.0
 HIGHEST = lax.Precision.HIGHEST
 BOTH = ("slab", "grp")
-VMEM_LIMIT = 64 * 1024 * 1024
+VMEM_LIMIT = 24 * 1024 * 1024
 F32, BF16 = jnp.float32, jnp.bfloat16
 
 
@@ -314,11 +314,33 @@
         return self._buffers[name]
 
 
-def call(body, ins, outs):
-    names, results = list(ins), list(outs)
-    pairs = [value if isinstance(value, tuple) else (value, ()) for value in ins.values()]
-    arrays = [array for array, _ in pairs]
-    copied = [place for place, (_, part) in enumerate(pairs) if part is not None]
+class Held:
+    def __init__(self, array):
+        self.array = array
+
+
+def call(body, ins, outs, keep=()):
+    names, results = list(ins), list(outs) + list(keep)
+    arrays, parts, copied = [], [], []
+    for place, value in enumerate(ins.values()):
+        held = isinstance(value, Held)
+        array, part = (value.array, None) if held else value if isinstance(value, tuple) else (value, ())
+        arrays.append(pltpu.with_memory_space_constraint(array, pltpu.VMEM if held else pltpu.HBM))
+        parts.append(part)
+        if part is not None:
+            copied.append(place)
+    kinds, sent = [], []
+    for place, value in enumerate(outs.values()):
+        if isinstance(value, Held):
+            kinds.append((value.array, F32))
+        else:
+            kinds.append(value if isinstance(value[-1], type(F32)) else (value, F32))
+            sent.append(place)
+    spaces = [
+        [pl.BlockSpec(memory_space=pltpu.VMEM if isinstance(value, Held) else pltpu.HBM) for value in side.values()]
+        for side in (ins, outs)
+    ]
+    spaces[1] += [pl.BlockSpec(memory_space=pltpu.VMEM)] * len(keep)
 
     def shape_of(array, part):
         if isinstance(part, str):
@@ -328,40 +350,52 @@
     def kernel(*refs):
         given, refs = refs[: len(names)], refs[len(names) :]
         made, refs = refs[: len(results)], refs[len(results) :]
-        held, refs = refs[: len(copied)], refs[len(copied) :]
-        built, (in_sems, out_sems) = refs[: len(results)], refs[len(results) :]
-        copies = {}
+        in_sems, out_sems = refs[-2:]
+        copies, buffers = {}, dict(zip(names, given))
         for slot, place in enumerate(copied):
-            part = pairs[place][1]
+            part = parts[place]
             origin = given[place].at[lax.axis_index(part) if isinstance(part, str) else part] if part else given[place]
-            copies[names[place]] = pltpu.make_async_copy(origin, held[slot], in_sems.at[slot])
-            copies[names[place]].start()
-        sent = []
-
-        def done(*buffers):
-            for buffer in buffers:
-                place = [other is buffer for other in built].index(True)
-                sent.append(pltpu.make_async_copy(buffer, made[place], out_sems.at[place]))
-                sent[-1].start()
-
-        get = Operands(copies, {names[place]: buffer for place, buffer in zip(copied, held)})
+            name = names[place]
+            buffers[name] = made[results.index(name, len(outs))] if name in keep else refs[slot]
+            copies[name] = pltpu.make_async_copy(origin, buffers[name], in_sems.at[slot])
+            copies[name].start()
+        built = list(made)
+        for slot, place in enumerate(sent):
+            built[place] = refs[len(copied) + slot]
+        going = []
+
+        def done(*which):
+            for buffer in which:
+                for slot, place in enumerate(sent):
+                    if built[place] is buffer:
+                        going.append(pltpu.make_async_copy(buffer, made[place], out_sems.at[slot]))
+                        going[-1].start()
+
+        get = Operands(copies, buffers)
         body(get, SimpleNamespace(**dict(zip(results, built))), done)
         for place in copied:
             getattr(get, names[place])
-        assert len(sent) == len(results)
-        for copy in sent:
+        assert len(going) == len(sent)
+        for copy in going:
             copy.wait()
 
-    kinds = [value if isinstance(value[-1], type(F32)) else (value, F32) for value in outs.values()]
-    buffers = [pltpu.VMEM(shape_of(*pairs[place]), arrays[place].dtype) for place in copied]
+    shapes = [(shape_of(arrays[place], parts[place]), arrays[place].dtype) for place in copied]
+    kept = [shapes[copied.index(names.index(name))] for name in keep]
+    scratch = [
+        pltpu.VMEM(*((8, 128), F32) if names[place] in keep else shape) for place, shape in zip(copied, shapes)
+    ]
+    scratch += [pltpu.VMEM(*kinds[place]) for place in sent]
+    scratch += [pltpu.SemaphoreType.DMA((max(1, len(some)),)) for some in (copied, sent)]
     made = pl.pallas_call(
         kernel,
-        out_shape=[jax.ShapeDtypeStruct(*kind) for kind in kinds],
-        in_specs=[pl.BlockSpec(memory_space=pl.ANY)] * len(names),
-        out_specs=[pl.BlockSpec(memory_space=pl.ANY)] * len(results),
-        scratch_shapes=buffers
-        + [pltpu.VMEM(*kind) for kind in kinds]
-        + [pltpu.SemaphoreType.DMA((len(copied),)), pltpu.SemaphoreType.DMA((len(results),))],
+        out_shape=[
+            pltpu.VMEM(*kind) if isinstance(value, Held) else pltpu.HBM(*kind)
+            for kind, value in zip(kinds, outs.values())
+        ]
+        + [pltpu.VMEM(*shape) for shape in kept],
+        in_specs=spaces[0],
+        out_specs=spaces[1],
+        scratch_shapes=scratch,
         compiler_params=pltpu.CompilerParams(vmem_limit_bytes=VMEM_LIMIT),
     )(*arrays)
     return SimpleNamespace(**dict(zip(results, made)))
@@ -446,22 +480,16 @@
         out.near[...], out.far[...] = choose(first, last)
         done(out.partial, out.near, out.far)
         first, last, left, right = rings(q_mixed, get)
-        line, chunk = out.line, out.chunk
-        line[:, :cols] = first
-        line[:, cols : 2 * cols] = last
-        line[:, at_zones:at_sides] = zone_line
-        west, east = side_lanes([rhs[layer] for layer in range(layers)], (left, right))
-        line[:, at_sides : at_sides + 128] = west
-        line[:, at_sides + 128 : at_sides + 256] = east
-        west, east = side_lanes(
+        sides = side_lanes([rhs[layer] for layer in range(layers)], (left, right))
+        sides += side_lanes(
             [cond[layer] for layer in range(layers)], (partial[0, :, 0:1], partial[0, :, cols - 1 : cols])
         )
-        line[:, at_sides + 256 : at_sides + 384] = west
-        line[:, at_sides + 384 : at_sides + 512] = east
         west, east = side_lanes([partial[layer] for layer in range(1, layers)])
-        line[:, at_sides + 512 :] = jnp.where(iota((1, 128), 1) < 64, west, pltpu.roll(east, 64, 1))
-        chunk[...] = jnp.broadcast_to(line[...][None], chunk.shape)
-        done(out.chunk, out.line)
+        both = jnp.where(iota((1, 128), 1) < 64, west, pltpu.roll(east, 64, 1))
+        line = jnp.concatenate([first, last, zone_line, *sides, both], axis=1)
+        out.chunk[...] = jnp.broadcast_to(line[None], out.chunk.shape)
+        out.zone_line[...] = zone_line
+        done(out.chunk)
 
     started = call(
         start_body,
@@ -481,18 +509,18 @@
             ends=t.ends,
         ),
         dict(
-            rhs=area,
-            q_mixed=(rows, cols),
+            rhs=Held(area),
+            q_mixed=Held((rows, cols)),
             partial=area,
             near=(3 * layers, cols),
             far=(3 * layers, cols),
-            line=(1, widths[0]),
+            zone_line=Held((1, blocks)),
             chunk=(devices, 1, widths[0]),
         ),
     )
     rhs = started.rhs
-    received = first_received = exchange(started.chunk)
-    near, far = first_near, first_far = neighbours(started.near, started.far)
+    received = exchange(started.chunk)
+    near, far = neighbours(started.near, started.far)
 
     def couple_body(get, out, done):
         ids, weights = get.pair_zones, get.pair_weight
@@ -502,14 +530,14 @@
         own = iota((zones, zones), 0) == iota((zones, zones), 1)
         matrix = matrix + jnp.where(own, get.zone_weight[...], 0.0)
         out.couple[...] = (COUPLE * zones / (slabs * rows * groups * cols)) * matrix
-        line = get.line[:, at_zones:at_sides].astype(jnp.int32)
+        line = get.zone_line[...].astype(jnp.int32)
         out.hot[...] = (iota((zones, blocks), 0) == line).astype(F32).astype(BF16)
         done(out.couple, out.hot)
 
     coupling = call(
         couple_body,
         dict(pair_zones=pair_zones.T, pair_weight=pair_weight[None], zone_weight=zone_weight[None])
-        | dict(line=started.line),
+        | dict(zone_line=Held(started.zone_line)),
         dict(couple=(zones, zones), hot=((zones, blocks), BF16)),
     )
     couple, hot = coupling.couple, coupling.hot
@@ -542,7 +570,7 @@
         if coupled:
             totals = jnp.sum(recv[:, 0, at_zones : at_zones + zones], axis=0, keepdims=True)
             reply = mm_f32(jnp.broadcast_to(totals, (8, zones)), get.couple[...])[0:1]
-            every = lookup(reply, get.zone_map[:, 0, :].astype(jnp.int32))
+            every = lookup(reply, get.zone_map[...].astype(jnp.int32))
             edges = edges + mm(every, get.coarse)
             share = 128 // block_cols
             inner = iota((devices, 128), 1) // block_cols
@@ -592,7 +620,7 @@
         north_ref, south_ref = choose(get.near[...], get.far[...])
         row, col = iota((rows, cols), 0), iota((rows, cols), 1)
         if coupled:
-            cond_north, cond_south = choose(get.first_near[...], get.first_far[...])
+            cond_north, cond_south = get.cond_north, get.cond_south
             sides = get.sides
             lanes = [of(-1, sides_at + 128), of(1, sides_at)]
             diagonal_ref, inverse_ref = get.diagonal, get.inverse
@@ -655,7 +683,9 @@
             sides[layers] = jnp.where(lane[:rows] == 0, ghosts[0][2], jnp.where(lane[:rows] == 1, ghosts[0][3], 0.0))
             beside[0:1] = ghosts[0][0]
             beside[1:2] = ghosts[0][1]
-            done(out.diagonal, out.inverse, out.sides, out.beside)
+            out.cond_north[...], out.cond_south[...] = north_ref[:layers], south_ref[:layers]
+            out.zone_map[...] = recv[:, 0, at_zones:at_sides]
+            done(out.diagonal, out.inverse, out.sides, out.beside, out.cond_north, out.cond_south, out.zone_map)
         v_out, image_out = out.v, out.image
         fields, outside = [], []
         for layer in range(layers):
@@ -705,7 +735,6 @@
             image_out[layer] = image
             images.append(image)
         done(out.image)
-        line, chunk = out.line, out.chunk
         totals = zone_totals(fields[0], get.hot[...], get.down[...])
         if final:
             rhs_ref, v0_ref, v1_ref, w0_ref = get.rhs, get.v0, get.v1, get.w0
@@ -724,8 +753,7 @@
             packed = jnp.zeros((1, 128), F32)
             for place, value in enumerate(products):
                 packed = jnp.where(iota((1, 128), 1) == place, value, packed)
-            line[:, :zones] = totals
-            line[:, zones:] = packed
+            line = jnp.concatenate([totals, packed], axis=1)
         else:
             depth = images[0]
             for layer in range(1, layers):
@@ -741,59 +769,56 @@
             done(out.near, out.far)
             first, last, left, right = rings(q_next, get)
             west, east = side_lanes(scaled, (left, right))
-            line[:, :cols] = first
-            line[:, cols : 2 * cols] = last
-            line[:, at_zones : at_zones + zones] = totals
-            line[:, at_zones + zones : at_zones + zones + 128] = west
-            line[:, at_zones + zones + 128 :] = east
-        chunk[...] = jnp.broadcast_to(line[...][None], chunk.shape)
-        done(out.chunk, out.line)
+            line = jnp.concatenate([first, last, totals, west, east], axis=1)
+        out.chunk[...] = jnp.broadcast_to(line[None], out.chunk.shape)
+        done(out.chunk)
 
     tail_width = zones + 128
     shared = {}
 
-    def step(number, received, q_mixed, w, near, far, more=()):
-        ins = dict(received=received)
+    def step(number, received, near, far, more, keep=()):
+        ins = dict(received=Held(received))
         if number > 0:
-            ins |= dict(couple=couple, zone_map=zone_map, coarse=t.coarse, up_modes=t.up_modes, coarse_rows=t.coarse_rows)
-        ins |= dict(row_chain=t.row_chain, answer=t.answer, q_mixed=q_mixed, w=w, down=t.down)
-        ins |= dict(waves=t.waves, own_columns=t.own_columns, around=t.around, wave_weight=t.wave_weight)
-        ins |= dict(ends=t.ends, sine_rows=t.sine_rows, weight=t.weight, sine_cols=t.sine_cols)
-        ins |= dict(near=near, far=far, conductivity=conductivity, leakance=leakance)
-        ins |= dict(hot=hot)
-        outs = dict(v=area, image=area)
-        if number > 0:
-            ins |= dict(first_near=first_near, first_far=first_far) | shared
+            ins |= dict(couple=couple, zone_map=one.zone_map, coarse=t.coarse, up_modes=t.up_modes)
+            ins |= dict(coarse_rows=t.coarse_rows)
+        ins |= dict(row_chain=t.row_chain, answer=t.answer, down=t.down, waves=t.waves, own_columns=t.own_columns)
+        ins |= dict(around=t.around, wave_weight=t.wave_weight, ends=t.ends, sine_rows=t.sine_rows, weight=t.weight)
+        ins |= dict(sine_cols=t.sine_cols, near=near, far=far, conductivity=conductivity, leakance=leakance, hot=hot)
+        ins |= shared | more
+        if number == 2:
+            outs = dict(v=Held(area), w=Held(area), image=Held(area))
+            outs |= dict(chunk=(devices, 1, tail_width))
+        else:
+            outs = dict(v=area, image=Held(area), q_mixed=Held((rows, cols)))
+            outs |= dict(near=(layers, cols), far=(layers, cols))
+            outs |= dict(chunk=(devices, 1, widths[1]))
+        if number == 0:
+            outs |= dict(diagonal=area, inverse=area, sides=(layers + 1, rows, 128), beside=(2, cols))
+            outs |= dict(cond_north=(layers, cols), cond_south=(layers, cols), zone_map=(devices, blocks))
+        elif number == 1:
             outs |= dict(w=area)
-        else:
-            ins |= dict(partial=started.partial, couple=(couple, None))
-            outs |= dict(diagonal=area, inverse=area, sides=(layers + 1, rows, 128), beside=(2, cols))
-        ins |= dict(more)
-        if number == 2:
-            outs |= dict(line=(1, tail_width), chunk=(devices, 1, tail_width))
-        else:
-            outs |= dict(
-                q_mixed=(rows, cols), near=(layers, cols), far=(layers, cols), line=(1, widths[1]), chunk=(devices, 1, widths[1])
-            )
-        return call(lambda get, out, done: step_body(number, get, out, done), ins, outs)
-
-    one = step(0, received, started.q_mixed, rhs, near, far)
-    shared.update(diagonal=one.diagonal, inverse=one.inverse, sides=one.sides, beside=one.beside)
-    zone_map = (first_received, (slice(None), slice(None), slice(at_zones, at_sides)))
+        return call(lambda get, out, done: step_body(number, get, out, done), ins, outs, keep)
+
+    q_mixed = Held(started.q_mixed)
+    one = step(0, received, near, far, dict(partial=started.partial, q_mixed=q_mixed, w=Held(rhs)))
+    shared |= dict(diagonal=one.diagonal, inverse=one.inverse, sides=one.sides, beside=one.beside)
+    shared |= dict(cond_north=one.cond_north, cond_south=one.cond_south)
     received = exchange(one.chunk)
     near, far = neighbours(one.near, one.far)
-    two = step(1, received, one.q_mixed, one.image, near, far)
+    two = step(1, received, near, far, dict(q_mixed=Held(one.q_mixed), w=Held(one.image)))
     received = exchange(two.chunk)
     near, far = neighbours(two.near, two.far)
-    more = dict(rhs=rhs, v0=one.v, v1=two.v, w0=two.w)
-    three = step(2, received, two.q_mixed, two.image, near, far, more)
+    more = dict(rhs=Held(rhs), v0=one.v, v1=two.v, w0=two.w)
+    after = dict(q_mixed=Held(two.q_mixed), w=Held(two.image)) | more
+    last_needs = tuple(dict(v0=0, v1=0, w0=0, couple=0, down=0))
+    three = step(2, received, near, far, after, last_needs)
     received = exchange(three.chunk)
 
     def finish_body(get, out, done):
         sums = jnp.sum(get.received[:, 0, :], axis=0, keepdims=True)
         totals = sums[:, :zones]
         reply = mm_f32(jnp.broadcast_to(totals, (8, zones)), get.couple[...])
-        zone_line = get.zone_line[:, at_zones:at_sides]
+        zone_line = get.zone_line[...]
         index = jnp.broadcast_to(zone_line, (8, blocks)).astype(jnp.int32)
         found = lookup(reply[0:1], index)[0:1]
         field = field_rows([(found, i) for i in range(block_rows)], get.down[...], block_cols)
@@ -817,10 +842,14 @@
             out.residual[layer] = rhs_ref[layer] - c0 * w0[layer] - c1 * w1[layer] - c2 * last
         done(out.solution, out.residual)
 
+    needs = {name: Held(getattr(three, name)) for name in last_needs}
+    for name, array in dict(couple=couple, down=t.down, v0=one.v, v1=two.v, w0=two.w).items():
+        needs.setdefault(name, array)
     ended = call(
         finish_body,
-        dict(received=received, couple=couple, zone_line=started.line, down=t.down)
-        | dict(rhs=rhs, v0=one.v, v1=two.v, v2=three.v, w0=two.w, w1=three.w, w2=three.image),
+        dict(received=Held(received), zone_line=Held(started.zone_line), rhs=Held(rhs))
+        | needs
+        | dict(v2=Held(three.v), w1=Held(three.w), w2=Held(three.image)),
         dict(solution=area, residual=area),
     )
     return ended.solution, ended.residual

time: 79.9 us -> 75.1 us (0.940)
  starting transfers between devices: 18.2 us -> 15.3 us
  Pallas kernels: 27.8 us -> 25.1 us
  waiting for transfers between devices: 22 us -> 23.3 us
    pallas_call x6, Pallas kernels: 27.8 us -> 25.1 us  [call(): pl.pallas_call(kernel, out_shape=[pltpu.VMEM(*kind) if isinstance(value,...]
    ppermute x3, starting transfers between devices: 3.75 us -> 1.95 us  [neighbours(): lax.ppermute(far, 'slab', across + [(j, i) for i, j in across])]
    all_to_all x3, starting transfers between devices: 14 us -> 12.5 us  [exchange(): return lax.all_to_all(chunk, BOTH, split_axis=0, concat_axis=0, tiled=True)]
  transfers between devices with their start and end apart: 9 -> 9, of which waited for: 3 -> 5; matrix products, arithmetic and copies ran while one was open for 0% -> 0% of each run, Pallas kernels for 3% -> 3%
where the time goes in v2:
time: 75.1 us; the launch traced here: 74.5 us
  Pallas kernels  25.1 us (33%)
  waiting for transfers between devices  23.3 us (31%)
  starting transfers between devices  15.3 us (20%)
  blocking collectives  9.96 us (13%)
  between operations  0.83 us (1%)
    pallas_call x6, Pallas kernels, call(): pl.pallas_call(kernel, out_shape=[pltpu.VMEM(*kind) if isinstance(value,...  25.1 us
    all_to_all x3, waiting for transfers between devices, exchange(): return lax.all_to_all(chunk, BOTH, split_axis=0, concat_axis=0, tiled=True)  22.7 us
    all_to_all x3, starting transfers between devices, exchange(): return lax.all_to_all(chunk, BOTH, split_axis=0, concat_axis=0, tiled=True)  12.5 us
    all_to_all x1, blocking collectives, exchange(): return lax.all_to_all(chunk, BOTH, split_axis=0, concat_axis=0, tiled=True)  9.96 us
    ppermute x3, starting transfers between devices, neighbours(): lax.ppermute(far, 'slab', across + [(j, i) for i, j in across])  1.95 us
  transfers between devices with their start and end apart: 9, of which 5 were waited for; matrix products, arithmetic and copies ran while one was open for 0% of the time, Pallas kernels for 3%

profile of v2, /device:TPU:0, one launch (start us, length us, event | category | flops | bytes accessed | tf_op | source)
XLA Modules:
  0.0 74.5 jit_solution(3362550707212643948)
XLA Ops:
  0.6 3.4 %shard_map.248 = (f32[3,32,512]{2,1,0:T(8,128)S(1)}, f32[32,512]{1,0:T(8,128)S(1)}, f32[3,32,512]{2,1,0:T(8,128)}, f32[9,512]{1,0:T(8,128)}, f32[9,512]{1,0:T(8,...) custom-call(s32[4,64]{1,0:T(4,128)} %refs_0_.1, f32[1,256]{1,0:T(1,128)} %bitcast.6, ...), custom_call_target="tpu_custom_call" | custom-call | tf_op jit(solution)/shard_map/pallas_call | solution.py:389
  4.1 0.0 copy-start.7
  4.1 7.3 %all-to-all-start = ((f32[32,1,1920]{2,1,0:T(1,128)}), f32[32,1,1920]{2,1,0:T(1,128)S(1)}, u32[]{:S(2)}, u32[]{:S(2)}) async-start(f32[32,1,1920]{2,1,0:T(1,128)} %get-tuple-element.40), calls=%async_computation | async-start | bytes 491520 | tf_op jit(solution)/shard_map/all_to_all | solution.py:442
  11.4 0.3 collective-permute-start
  11.7 0.7 collective-permute-start.1
  12.4 2.4 %shard_map.249 = (f32[256,256]{1,0:T(8,128)}, bf16[256,256]{1,0:T(8,128)(2,1)}) custom-call(s32[2,512]{1,0:T(2,128)} %bitcast.4, f32[1,512]{1,0:T(1,128)} %bitcast.5, f32[1,256]{1,0:T(1,128)} %bitcast.7, f32[1,256]{1,0:T(1,128)S(1)} %get-tuple-element.43.refs_3_.refs_1_), custom_call_target="tpu_custom_call" | custom-call | tf_op jit(solution)/shard_map/pallas_call | solution.py:389
  14.8 0.0 collective-permute-done.1.refs_13_
  14.9 6.5 %all-to-all-done.refs_0_ = f32[32,1,1920]{2,1,0:T(1,128)S(1)} async-done(((f32[32,1,1920]{2,1,0:T(1,128)}), f32[32,1,1920]{2,1,0:T(1,128)S(1)}, u32[]{:S(2)}, u32[]{:S(2)}) %all-to-all-start) | async-done | bytes 245792 | tf_op jit(solution)/shard_map/all_to_all | solution.py:442
  21.4 5.3 %shard_map.250 = (f32[3,32,512]{2,1,0:T(8,128)}, f32[3,32,512]{2,1,0:T(8,128)S(1)}, f32[32,512]{1,0:T(8,128)S(1)}, f32[3,512]{1,0:T(4,128)}, f32[3,512]{1,0:T(4,...) custom-call(f32[32,1,1920]{2,1,0:T(1,128)S(1)} %all-to-all-done.refs, ...), custom_call_target="tpu_custom_call" | custom-call | tf_op jit(solution)/shard_map/pallas_call | solution.py:389
  26.7 2.6 %all-to-all-start.1 = ((f32[32,1,1536]{2,1,0:T(1,128)}), f32[32,1,1536]{2,1,0:T(1,128)S(1)}, u32[]{:S(2)}, u32[]{:S(2)}) async-start(f32[32,1,1536]{2,1,0:T(1,128)} %get-tuple-element.48), calls=%async_computation.1 | async-start | bytes 393216 | tf_op jit(solution)/shard_map/all_to_all | solution.py:442
  29.3 0.3 collective-permute-start.2
  29.6 0.7 collective-permute-start.3
  30.3 0.3 collective-permute-done.2.refs_17_
  30.6 0.0 collective-permute-done.3.refs_18_
  30.6 8.1 %all-to-all-done.1.refs_0_ = f32[32,1,1536]{2,1,0:T(1,128)S(1)} async-done(((f32[32,1,1536]{2,1,0:T(1,128)}), f32[32,1,1536]{2,1,0:T(1,128)S(1)}, u32[]{:S(2)}, u32[]{:S(2)}) %all-to-all-start.1) | async-done | bytes 196640 | tf_op jit(solution)/shard_map/all_to_all | solution.py:442
  38.6 6.3 %shard_map.251 = (f32[3,32,512]{2,1,0:T(8,128)}, f32[3,32,512]{2,1,0:T(8,128)S(1)}, f32[32,512]{1,0:T(8,128)S(1)}, f32[3,512]{1,0:T(4,128)}, f32[3,512]{1,0:T(4,...) custom-call(f32[32,1,1536]{2,1,0:T(1,128)S(1)} %all-to-all-done.1.refs_0_, f32[256,256]{1,0:T(8,128)} %get-tuple-element.49.refs_1_, ...), custom_call_target="tpu_custom_call" | custom-call | tf_op jit(solution)/shard_map/pallas_call | solution.py:389
  45.0 2.6 %all-to-all-start.2 = ((f32[32,1,1536]{2,1,0:T(1,128)}), f32[32,1,1536]{2,1,0:T(1,128)S(1)}, u32[]{:S(2)}, u32[]{:S(2)}) async-start(f32[32,1,1536]{2,1,0:T(1,128)} %get-tuple-element.61), calls=%async_computation.2 | async-start | bytes 393216 | tf_op jit(solution)/shard_map/all_to_all | solution.py:442
  47.6 0.2 collective-permute-start.4
  47.9 0.7 collective-permute-start.5
  48.5 0.3 collective-permute-done.4.refs_17_
  48.9 8.1 %all-to-all-done.2.refs_0_ = f32[32,1,1536]{2,1,0:T(1,128)S(1)} async-done(((f32[32,1,1536]{2,1,0:T(1,128)}), f32[32,1,1536]{2,1,0:T(1,128)S(1)}, u32[]{:S(2)}, u32[]{:S(2)}) %all-to-all-start.2) | async-done | bytes 196640 | tf_op jit(solution)/shard_map/all_to_all | solution.py:442
  57.0 5.9 %shard_map.252 = (f32[3,32,512]{2,1,0:T(8,128)S(1)}, f32[3,32,512]{2,1,0:T(8,128)S(1)}, f32[3,32,512]{2,1,0:T(8,128)S(1)}, f32[32,1,384]{2,1,0:T(1,128)}, f32[3,...) custom-call(f32[32,1,1536]{2,1,0:T(1,128)S(1)} %all-to-all-done.2.re, ...), custom_call_target="tpu_custom_call" | custom-call | tf_op jit(solution)/shard_map/pallas_call | solution.py:389
  62.9 10.0 %all_to_all.20.refs_0_ = f32[32,1,384]{2,1,0:T(1,128)S(1)} all-to-all(f32[32,1,384]{2,1,0:T(1,128)} %get-tuple-element.69), channel_id=1, replica_groups=mesh['slab'=8,'grp'=4] {'slab','grp'}, dimensions={0} | all-to-all | bytes 98304 | tf_op jit(solution)/shard_map/all_to_all | solution.py:442
  72.8 1.7 %shard_map.253 = (f32[3,32,512]{2,1,0:T(8,128)}, f32[3,32,512]{2,1,0:T(8,128)}) custom-call(f32[32,1,384]{2,1,0:T(1,128)S(1)} %all_to_all.20.refs_0_, f32[1,256]{1,0:T(1,128)S(1)} %get-tuple-element.43.refs_3_.refs_1_, f32[3,32,512]{2,1,0:T(8,128)S(1)} %get-tuple-element.47.refs_19_.refs_30_.refs_2_, f32[3,32,512]{2,1,0:T(8,128)S(1)} %get-tuple-element.70.refs_3_, ...), custom_call_target="tpu_custom_call" | custom-call | tf_op jit(solution)/shard_map/pallas_call | solution.py:389
  (25 shorter events, 0.1 us)
Async XLA Ops:
  4.1 7.3 %copy-start.7 = (f32[9,512]{1,0:T(8,128)S(1)}, f32[9,512]{1,0:T(8,128)}, u32[]{:S(2)}) copy-start(f32[9,512]{1,0:T(8,128)} %get-tuple-element.41) | copy-start | bytes 55300
  4.1 7.7 %copy-start.6 = (f32[9,512]{1,0:T(8,128)S(1)}, f32[9,512]{1,0:T(8,128)}, u32[]{:S(2)}) copy-start(f32[9,512]{1,0:T(8,128)} %get-tuple-element.42) | copy-start | bytes 55300
  4.1 17.3 %all-to-all-start = ((f32[32,1,1920]{2,1,0:T(1,128)}), f32[32,1,1920]{2,1,0:T(1,128)S(1)}, u32[]{:S(2)}, u32[]{:S(2)}) async-start(f32[32,1,1920]{2,1,0:T(1,128)} %get-tuple-element.40), calls=%async_computation | async-start | bytes 491520 | tf_op jit(solution)/shard_map/all_to_all | solution.py:442
  11.4 3.4 %collective-permute-start = (f32[9,512]{1,0:T(8,128)S(1)}, f32[9,512]{1,0:T(8,128)S(1)}, u32[]{:S(2)}, u32[]{:S(2)}) collective-permute-start(f32[9,512]{1,0:T(8,128)S(1)} %copy-done.7), channel_id=1, source_target_pairs={{0,4},{4,0},{8,12},{12,8},{16,20},{20,16},{24,28},{28,24},{1,5},{5... | collective-permute-start | bytes 55304 | tf_op jit(solution)/shard_map/ppermute | solution.py:433
  11.7 3.1 %collective-permute-start.1 = (f32[9,512]{1,0:T(8,128)S(1)}, f32[9,512]{1,0:T(8,128)S(1)}, u32[]{:S(2)}, u32[]{:S(2)}) collective-permute-start(f32[9,512]{1,0:T(8,128)S(1)} %copy-done.6), channel_id=1, source_target_pairs={{4,8},{12,16},{20,24},{8,4},{16,12},{24,20},{5,9},{13,17},{21,25},... | collective-permute-start | bytes 55304 | tf_op jit(solution)/shard_map/ppermute | solution.py:434
  14.8 6.6 %copy-start = (f32[9,512]{1,0:T(8,128)}, f32[9,512]{1,0:T(8,128)S(1)}, u32[]{:S(2)}) copy-start(f32[9,512]{1,0:T(8,128)S(1)} %collective-permute-done.refs_12_) | copy-start | bytes 55300
  14.8 6.6 %copy-start.1 = (f32[9,512]{1,0:T(8,128)}, f32[9,512]{1,0:T(8,128)S(1)}, u32[]{:S(2)}) copy-start(f32[9,512]{1,0:T(8,128)S(1)} %collective-permute-done.1.refs_13_) | copy-start | bytes 55300
  26.7 2.6 %copy-start.9 = (f32[3,512]{1,0:T(4,128)S(1)}, f32[3,512]{1,0:T(4,128)}, u32[]{:S(2)}) copy-start(f32[3,512]{1,0:T(4,128)} %get-tuple-element.51) | copy-start | bytes 18436
  26.7 2.9 %copy-start.8 = (f32[3,512]{1,0:T(4,128)S(1)}, f32[3,512]{1,0:T(4,128)}, u32[]{:S(2)}) copy-start(f32[3,512]{1,0:T(4,128)} %get-tuple-element.52) | copy-start | bytes 18436
  26.7 11.9 %all-to-all-start.1 = ((f32[32,1,1536]{2,1,0:T(1,128)}), f32[32,1,1536]{2,1,0:T(1,128)S(1)}, u32[]{:S(2)}, u32[]{:S(2)}) async-start(f32[32,1,1536]{2,1,0:T(1,128)} %get-tuple-element.48), calls=%async_computation.1 | async-start | bytes 393216 | tf_op jit(solution)/shard_map/all_to_all | solution.py:442
  29.3 1.2 %collective-permute-start.2 = (f32[3,512]{1,0:T(4,128)S(1)}, f32[3,512]{1,0:T(4,128)S(1)}, u32[]{:S(2)}, u32[]{:S(2)}) collective-permute-start(f32[3,512]{1,0:T(4,128)S(1)} %copy-done.9), channel_id=1, source_target_pairs={{0,4},{4,0},{8,12},{12,8},{16,20},{20,16},{24,28},{28,24},{1,5},{5... | collective-permute-start | bytes 18440 | tf_op jit(solution)/shard_map/ppermute | solution.py:433
  29.6 0.9 %collective-permute-start.3 = (f32[3,512]{1,0:T(4,128)S(1)}, f32[3,512]{1,0:T(4,128)S(1)}, u32[]{:S(2)}, u32[]{:S(2)}) collective-permute-start(f32[3,512]{1,0:T(4,128)S(1)} %copy-done.8), channel_id=1, source_target_pairs={{4,8},{12,16},{20,24},{8,4},{16,12},{24,20},{5,9},{13,17},{21,25},... | collective-permute-start | bytes 18440 | tf_op jit(solution)/shard_map/ppermute | solution.py:434
  30.6 8.1 %copy-start.4 = (f32[3,512]{1,0:T(4,128)}, f32[3,512]{1,0:T(4,128)S(1)}, u32[]{:S(2)}) copy-start(f32[3,512]{1,0:T(4,128)S(1)} %collective-permute-done.2.refs_17_) | copy-start | bytes 18436
  30.6 8.1 %copy-start.5 = (f32[3,512]{1,0:T(4,128)}, f32[3,512]{1,0:T(4,128)S(1)}, u32[]{:S(2)}) copy-start(f32[3,512]{1,0:T(4,128)S(1)} %collective-permute-done.3.refs_18_) | copy-start | bytes 18436
  45.0 2.6 %copy-start.11 = (f32[3,512]{1,0:T(4,128)S(1)}, f32[3,512]{1,0:T(4,128)}, u32[]{:S(2)}) copy-start(f32[3,512]{1,0:T(4,128)} %get-tuple-element.62) | copy-start | bytes 18436
  45.0 2.9 %copy-start.10 = (f32[3,512]{1,0:T(4,128)S(1)}, f32[3,512]{1,0:T(4,128)}, u32[]{:S(2)}) copy-start(f32[3,512]{1,0:T(4,128)} %get-tuple-element.63) | copy-start | bytes 18436
  45.0 11.9 %all-to-all-start.2 = ((f32[32,1,1536]{2,1,0:T(1,128)}), f32[32,1,1536]{2,1,0:T(1,128)S(1)}, u32[]{:S(2)}, u32[]{:S(2)}) async-start(f32[32,1,1536]{2,1,0:T(1,128)} %get-tuple-element.61), calls=%async_computation.2 | async-start | bytes 393216 | tf_op jit(solution)/shard_map/all_to_all | solution.py:442
  47.6 1.2 %collective-permute-start.4 = (f32[3,512]{1,0:T(4,128)S(1)}, f32[3,512]{1,0:T(4,128)S(1)}, u32[]{:S(2)}, u32[]{:S(2)}) collective-permute-start(f32[3,512]{1,0:T(4,128)S(1)} %copy-done.11), channel_id=1, source_target_pairs={{0,4},{4,0},{8,12},{12,8},{16,20},{20,16},{24,28},{28,24},{1,5},{5... | collective-permute-start | bytes 18440 | tf_op jit(solution)/shard_map/ppermute | solution.py:433
  47.9 1.0 %collective-permute-start.5 = (f32[3,512]{1,0:T(4,128)S(1)}, f32[3,512]{1,0:T(4,128)S(1)}, u32[]{:S(2)}, u32[]{:S(2)}) collective-permute-start(f32[3,512]{1,0:T(4,128)S(1)} %copy-done.10), channel_id=1, source_target_pairs={{4,8},{12,16},{20,24},{8,4},{16,12},{24,20},{5,9},{13,17},{21,25},... | collective-permute-start | bytes 18440 | tf_op jit(solution)/shard_map/ppermute | solution.py:434
  48.9 8.1 %copy-start.2 = (f32[3,512]{1,0:T(4,128)}, f32[3,512]{1,0:T(4,128)S(1)}, u32[]{:S(2)}) copy-start(f32[3,512]{1,0:T(4,128)S(1)} %collective-permute-done.4.refs_17_) | copy-start | bytes 18436
  48.9 8.1 %copy-start.3 = (f32[3,512]{1,0:T(4,128)}, f32[3,512]{1,0:T(4,128)S(1)}, u32[]{:S(2)}) copy-start(f32[3,512]{1,0:T(4,128)S(1)} %collective-permute-done.5.refs_18_) | copy-start | bytes 18436

commit v3 on v2

--- a/solution.py
+++ b/solution.py
@@ -305,12 +305,15 @@
 
 
 class Operands:
-    def __init__(self, copies, buffers):
-        self._copies, self._buffers = copies, buffers
+    def __init__(self, copies, buffers, early):
+        self._copies, self._buffers, self._early = copies, buffers, early
 
     def __getattr__(self, name):
         if name in self._copies:
-            self._copies.pop(name).wait()
+            names = list(self._copies)
+            for other in names if name not in names[: self._early] else names[: self._early]:
+                self._copies.pop(other).wait()
+            self._early = 0
         return self._buffers[name]
 
 
@@ -319,7 +322,7 @@
         self.array = array
 
 
-def call(body, ins, outs, keep=()):
+def call(body, ins, outs, keep=(), early=0):
     names, results = list(ins), list(outs) + list(keep)
     arrays, parts, copied = [], [], []
     for place, value in enumerate(ins.values()):
@@ -371,7 +374,7 @@
                         going.append(pltpu.make_async_copy(buffer, made[place], out_sems.at[slot]))
                         going[-1].start()
 
-        get = Operands(copies, buffers)
+        get = Operands(copies, buffers, early)
         body(get, SimpleNamespace(**dict(zip(results, built))), done)
         for place in copied:
             getattr(get, names[place])
@@ -517,6 +520,7 @@
             zone_line=Held((1, blocks)),
             chunk=(devices, 1, widths[0]),
         ),
+        early=4,
     )
     rhs = started.rhs
     received = exchange(started.chunk)
@@ -785,6 +789,7 @@
         ins |= dict(around=t.around, wave_weight=t.wave_weight, ends=t.ends, sine_rows=t.sine_rows, weight=t.weight)
         ins |= dict(sine_cols=t.sine_cols, near=near, far=far, conductivity=conductivity, leakance=leakance, hot=hot)
         ins |= shared | more
+        ins |= {name: Held(getattr(one, name)) for name in steady} if number else {}
         if number == 2:
             outs = dict(v=Held(area), w=Held(area), image=Held(area))
             outs |= dict(chunk=(devices, 1, tail_width))
@@ -797,10 +802,11 @@
             outs |= dict(cond_north=(layers, cols), cond_south=(layers, cols), zone_map=(devices, blocks))
         elif number == 1:
             outs |= dict(w=area)
-        return call(lambda get, out, done: step_body(number, get, out, done), ins, outs, keep)
+        return call(lambda get, out, done: step_body(number, get, out, done), ins, outs, keep, early=5)
 
     q_mixed = Held(started.q_mixed)
-    one = step(0, received, near, far, dict(partial=started.partial, q_mixed=q_mixed, w=Held(rhs)))
+    steady = tuple(dict(sine_cols=0, wave_weight=0))
+    one = step(0, received, near, far, dict(partial=started.partial, q_mixed=q_mixed, w=Held(rhs)), steady)
     shared |= dict(diagonal=one.diagonal, inverse=one.inverse, sides=one.sides, beside=one.beside)
     shared |= dict(cond_north=one.cond_north, cond_south=one.cond_south)
     received = exchange(one.chunk)

time: 75.1 us -> 72.5 us (0.965)
  Pallas kernels: 25.1 us -> 22.3 us
    pallas_call x6, Pallas kernels: 25.1 us -> 22.3 us  [call(): pl.pallas_call(kernel, out_shape=[pltpu.VMEM(*kind) if isinstance(value,...]
where the time goes in v3:
time: 72.5 us; the launch traced here: 71.9 us
  waiting for transfers between devices  23.5 us (32%)
  Pallas kernels  22.3 us (31%)
  starting transfers between devices  15.3 us (21%)
  blocking collectives  9.96 us (14%)
  between operations  0.83 us (1%)
    all_to_all x3, waiting for transfers between devices, exchange(): return lax.all_to_all(chunk, BOTH, split_axis=0, concat_axis=0, tiled=True)  22.8 us
    pallas_call x6, Pallas kernels, call(): pl.pallas_call(kernel, out_shape=[pltpu.VMEM(*kind) if isinstance(value,...  22.3 us
    all_to_all x3, starting transfers between devices, exchange(): return lax.all_to_all(chunk, BOTH, split_axis=0, concat_axis=0, tiled=True)  12.5 us
    all_to_all x1, blocking collectives, exchange(): return lax.all_to_all(chunk, BOTH, split_axis=0, concat_axis=0, tiled=True)  9.96 us
    ppermute x3, starting transfers between devices, neighbours(): lax.ppermute(far, 'slab', across + [(j, i) for i, j in across])  1.95 us
  transfers between devices with their start and end apart: 9, of which 5 were waited for; matrix products, arithmetic and copies ran while one was open for 0% of the time, Pallas kernels for 3%

profile of v3, /device:TPU:0, one launch (start us, length us, event | category | flops | bytes accessed | tf_op | source)
XLA Modules:
  0.0 71.9 jit_solution(14750681821759709654)
XLA Ops:
  0.6 3.2 %shard_map.248 = (f32[3,32,512]{2,1,0:T(8,128)S(1)}, f32[32,512]{1,0:T(8,128)S(1)}, f32[3,32,512]{2,1,0:T(8,128)}, f32[9,512]{1,0:T(8,128)}, f32[9,512]{1,0:T(8,...) custom-call(s32[4,64]{1,0:T(4,128)} %refs_0_.1, f32[1,256]{1,0:T(1,128)} %bitcast.6, ...), custom_call_target="tpu_custom_call" | custom-call | tf_op jit(solution)/shard_map/pallas_call | solution.py:392
  3.9 0.0 copy-start.7
  3.9 7.3 %all-to-all-start = ((f32[32,1,1920]{2,1,0:T(1,128)}), f32[32,1,1920]{2,1,0:T(1,128)S(1)}, u32[]{:S(2)}, u32[]{:S(2)}) async-start(f32[32,1,1920]{2,1,0:T(1,128)} %get-tuple-element.42), calls=%async_computation | async-start | bytes 491520 | tf_op jit(solution)/shard_map/all_to_all | solution.py:445
  11.2 0.3 collective-permute-start
  11.5 0.7 collective-permute-start.1
  12.2 2.3 %shard_map.249 = (f32[256,256]{1,0:T(8,128)}, bf16[256,256]{1,0:T(8,128)(2,1)}) custom-call(s32[2,512]{1,0:T(2,128)} %bitcast.4, f32[1,512]{1,0:T(1,128)} %bitcast.5, f32[1,256]{1,0:T(1,128)} %bitcast.7, f32[1,256]{1,0:T(1,128)S(1)} %get-tuple-element.45.refs_3_.refs_1_), custom_call_target="tpu_custom_call" | custom-call | tf_op jit(solution)/shard_map/pallas_call | solution.py:392
  14.5 0.0 collective-permute-done.refs_12_
  14.5 0.0 collective-permute-done.1.refs_13_
  14.5 6.7 %all-to-all-done.refs_0_ = f32[32,1,1920]{2,1,0:T(1,128)S(1)} async-done(((f32[32,1,1920]{2,1,0:T(1,128)}), f32[32,1,1920]{2,1,0:T(1,128)S(1)}, u32[]{:S(2)}, u32[]{:S(2)}) %all-to-all-start) | async-done | bytes 245792 | tf_op jit(solution)/shard_map/all_to_all | solution.py:445
  21.2 4.9 %shard_map.250 = (f32[3,32,512]{2,1,0:T(8,128)}, f32[3,32,512]{2,1,0:T(8,128)S(1)}, f32[32,512]{1,0:T(8,128)S(1)}, f32[3,512]{1,0:T(4,128)}, f32[3,512]{1,0:T(4,...) custom-call(f32[32,1,1920]{2,1,0:T(1,128)S(1)} %all-to-all-done.refs, ...), custom_call_target="tpu_custom_call" | custom-call | tf_op jit(solution)/shard_map/pallas_call | solution.py:392
  26.1 2.6 %all-to-all-start.1 = ((f32[32,1,1536]{2,1,0:T(1,128)}), f32[32,1,1536]{2,1,0:T(1,128)S(1)}, u32[]{:S(2)}, u32[]{:S(2)}) async-start(f32[32,1,1536]{2,1,0:T(1,128)} %get-tuple-element.50), calls=%async_computation.1 | async-start | bytes 393216 | tf_op jit(solution)/shard_map/all_to_all | solution.py:445
  28.7 0.3 collective-permute-start.2
  29.0 0.7 collective-permute-start.3
  29.7 0.3 collective-permute-done.2.refs_17_
  29.9 8.1 %all-to-all-done.1.refs_0_ = f32[32,1,1536]{2,1,0:T(1,128)S(1)} async-done(((f32[32,1,1536]{2,1,0:T(1,128)}), f32[32,1,1536]{2,1,0:T(1,128)S(1)}, u32[]{:S(2)}, u32[]{:S(2)}) %all-to-all-start.1) | async-done | bytes 196640 | tf_op jit(solution)/shard_map/all_to_all | solution.py:445
  38.0 5.4 %shard_map.251 = (f32[3,32,512]{2,1,0:T(8,128)}, f32[3,32,512]{2,1,0:T(8,128)S(1)}, f32[32,512]{1,0:T(8,128)S(1)}, f32[3,512]{1,0:T(4,128)}, f32[3,512]{1,0:T(4,...) custom-call(f32[32,1,1536]{2,1,0:T(1,128)S(1)} %all-to-all-done.1.refs_0_, f32[256,256]{1,0:T(8,128)} %get-tuple-element.51.refs_1_, ...), custom_call_target="tpu_custom_call" | custom-call | tf_op jit(solution)/shard_map/pallas_call | solution.py:392
  43.5 2.6 %all-to-all-start.2 = ((f32[32,1,1536]{2,1,0:T(1,128)}), f32[32,1,1536]{2,1,0:T(1,128)S(1)}, u32[]{:S(2)}, u32[]{:S(2)}) async-start(f32[32,1,1536]{2,1,0:T(1,128)} %get-tuple-element.65), calls=%async_computation.2 | async-start | bytes 393216 | tf_op jit(solution)/shard_map/all_to_all | solution.py:445
  46.1 0.2 collective-permute-start.4
  46.3 0.7 collective-permute-start.5
  47.0 0.3 collective-permute-done.4.refs_17_
  47.3 8.1 %all-to-all-done.2.refs_0_ = f32[32,1,1536]{2,1,0:T(1,128)S(1)} async-done(((f32[32,1,1536]{2,1,0:T(1,128)}), f32[32,1,1536]{2,1,0:T(1,128)S(1)}, u32[]{:S(2)}, u32[]{:S(2)}) %all-to-all-start.2) | async-done | bytes 196640 | tf_op jit(solution)/shard_map/all_to_all | solution.py:445
  55.4 4.9 %shard_map.252 = (f32[3,32,512]{2,1,0:T(8,128)S(1)}, f32[3,32,512]{2,1,0:T(8,128)S(1)}, f32[3,32,512]{2,1,0:T(8,128)S(1)}, f32[32,1,384]{2,1,0:T(1,128)}, f32[3,...) custom-call(f32[32,1,1536]{2,1,0:T(1,128)S(1)} %all-to-all-done.2.re, ...), custom_call_target="tpu_custom_call" | custom-call | tf_op jit(solution)/shard_map/pallas_call | solution.py:392
  60.3 10.0 %all_to_all.20.refs_0_ = f32[32,1,384]{2,1,0:T(1,128)S(1)} all-to-all(f32[32,1,384]{2,1,0:T(1,128)} %get-tuple-element.73), channel_id=1, replica_groups=mesh['slab'=8,'grp'=4] {'slab','grp'}, dimensions={0} | all-to-all | bytes 98304 | tf_op jit(solution)/shard_map/all_to_all | solution.py:445
  70.2 1.7 %shard_map.253 = (f32[3,32,512]{2,1,0:T(8,128)}, f32[3,32,512]{2,1,0:T(8,128)}) custom-call(f32[32,1,384]{2,1,0:T(1,128)S(1)} %all_to_all.20.refs_0_, f32[1,256]{1,0:T(1,128)S(1)} %get-tuple-element.45.refs_3_.refs_1_, f32[3,32,512]{2,1,0:T(8,128)S(1)} %get-tuple-element.49.refs_19_.refs_30_.refs_2_, f32[3,32,512]{2,1,0:T(8,128)S(1)} %get-tuple-element.74.refs_3_, ...), custom_call_target="tpu_custom_call" | custom-call | tf_op jit(solution)/shard_map/pallas_call | solution.py:392
  (25 shorter events, 0.1 us)
Async XLA Ops:
  3.9 7.3 %copy-start.7 = (f32[9,512]{1,0:T(8,128)S(1)}, f32[9,512]{1,0:T(8,128)}, u32[]{:S(2)}) copy-start(f32[9,512]{1,0:T(8,128)} %get-tuple-element.43) | copy-start | bytes 55300
  3.9 7.7 %copy-start.6 = (f32[9,512]{1,0:T(8,128)S(1)}, f32[9,512]{1,0:T(8,128)}, u32[]{:S(2)}) copy-start(f32[9,512]{1,0:T(8,128)} %get-tuple-element.44) | copy-start | bytes 55300
  3.9 17.3 %all-to-all-start = ((f32[32,1,1920]{2,1,0:T(1,128)}), f32[32,1,1920]{2,1,0:T(1,128)S(1)}, u32[]{:S(2)}, u32[]{:S(2)}) async-start(f32[32,1,1920]{2,1,0:T(1,128)} %get-tuple-element.42), calls=%async_computation | async-start | bytes 491520 | tf_op jit(solution)/shard_map/all_to_all | solution.py:445
  11.2 3.3 %collective-permute-start = (f32[9,512]{1,0:T(8,128)S(1)}, f32[9,512]{1,0:T(8,128)S(1)}, u32[]{:S(2)}, u32[]{:S(2)}) collective-permute-start(f32[9,512]{1,0:T(8,128)S(1)} %copy-done.7), channel_id=1, source_target_pairs={{0,4},{4,0},{8,12},{12,8},{16,20},{20,16},{24,28},{28,24},{1,5},{5... | collective-permute-start | bytes 55304 | tf_op jit(solution)/shard_map/ppermute | solution.py:436
  11.5 3.0 %collective-permute-start.1 = (f32[9,512]{1,0:T(8,128)S(1)}, f32[9,512]{1,0:T(8,128)S(1)}, u32[]{:S(2)}, u32[]{:S(2)}) collective-permute-start(f32[9,512]{1,0:T(8,128)S(1)} %copy-done.6), channel_id=1, source_target_pairs={{4,8},{12,16},{20,24},{8,4},{16,12},{24,20},{5,9},{13,17},{21,25},... | collective-permute-start | bytes 55304 | tf_op jit(solution)/shard_map/ppermute | solution.py:437
  14.5 6.7 %copy-start = (f32[9,512]{1,0:T(8,128)}, f32[9,512]{1,0:T(8,128)S(1)}, u32[]{:S(2)}) copy-start(f32[9,512]{1,0:T(8,128)S(1)} %collective-permute-done.refs_12_) | copy-start | bytes 55300
  14.5 6.7 %copy-start.1 = (f32[9,512]{1,0:T(8,128)}, f32[9,512]{1,0:T(8,128)S(1)}, u32[]{:S(2)}) copy-start(f32[9,512]{1,0:T(8,128)S(1)} %collective-permute-done.1.refs_13_) | copy-start | bytes 55300
  26.1 2.6 %copy-start.9 = (f32[3,512]{1,0:T(4,128)S(1)}, f32[3,512]{1,0:T(4,128)}, u32[]{:S(2)}) copy-start(f32[3,512]{1,0:T(4,128)} %get-tuple-element.55) | copy-start | bytes 18436
  26.1 2.9 %copy-start.8 = (f32[3,512]{1,0:T(4,128)S(1)}, f32[3,512]{1,0:T(4,128)}, u32[]{:S(2)}) copy-start(f32[3,512]{1,0:T(4,128)} %get-tuple-element.56) | copy-start | bytes 18436
  26.1 11.9 %all-to-all-start.1 = ((f32[32,1,1536]{2,1,0:T(1,128)}), f32[32,1,1536]{2,1,0:T(1,128)S(1)}, u32[]{:S(2)}, u32[]{:S(2)}) async-start(f32[32,1,1536]{2,1,0:T(1,128)} %get-tuple-element.50), calls=%async_computation.1 | async-start | bytes 393216 | tf_op jit(solution)/shard_map/all_to_all | solution.py:445
  28.7 1.2 %collective-permute-start.2 = (f32[3,512]{1,0:T(4,128)S(1)}, f32[3,512]{1,0:T(4,128)S(1)}, u32[]{:S(2)}, u32[]{:S(2)}) collective-permute-start(f32[3,512]{1,0:T(4,128)S(1)} %copy-done.9), channel_id=1, source_target_pairs={{0,4},{4,0},{8,12},{12,8},{16,20},{20,16},{24,28},{28,24},{1,5},{5... | collective-permute-start | bytes 18440 | tf_op jit(solution)/shard_map/ppermute | solution.py:436
  29.0 0.9 %collective-permute-start.3 = (f32[3,512]{1,0:T(4,128)S(1)}, f32[3,512]{1,0:T(4,128)S(1)}, u32[]{:S(2)}, u32[]{:S(2)}) collective-permute-start(f32[3,512]{1,0:T(4,128)S(1)} %copy-done.8), channel_id=1, source_target_pairs={{4,8},{12,16},{20,24},{8,4},{16,12},{24,20},{5,9},{13,17},{21,25},... | collective-permute-start | bytes 18440 | tf_op jit(solution)/shard_map/ppermute | solution.py:437
  29.9 8.1 %copy-start.4 = (f32[3,512]{1,0:T(4,128)}, f32[3,512]{1,0:T(4,128)S(1)}, u32[]{:S(2)}) copy-start(f32[3,512]{1,0:T(4,128)S(1)} %collective-permute-done.2.refs_17_) | copy-start | bytes 18436
  29.9 8.1 %copy-start.5 = (f32[3,512]{1,0:T(4,128)}, f32[3,512]{1,0:T(4,128)S(1)}, u32[]{:S(2)}) copy-start(f32[3,512]{1,0:T(4,128)S(1)} %collective-permute-done.3.refs_18_) | copy-start | bytes 18436
  43.5 2.6 %copy-start.11 = (f32[3,512]{1,0:T(4,128)S(1)}, f32[3,512]{1,0:T(4,128)}, u32[]{:S(2)}) copy-start(f32[3,512]{1,0:T(4,128)} %get-tuple-element.66) | copy-start | bytes 18436
  43.5 2.9 %copy-start.10 = (f32[3,512]{1,0:T(4,128)S(1)}, f32[3,512]{1,0:T(4,128)}, u32[]{:S(2)}) copy-start(f32[3,512]{1,0:T(4,128)} %get-tuple-element.67) | copy-start | bytes 18436
  43.5 11.9 %all-to-all-start.2 = ((f32[32,1,1536]{2,1,0:T(1,128)}), f32[32,1,1536]{2,1,0:T(1,128)S(1)}, u32[]{:S(2)}, u32[]{:S(2)}) async-start(f32[32,1,1536]{2,1,0:T(1,128)} %get-tuple-element.65), calls=%async_computation.2 | async-start | bytes 393216 | tf_op jit(solution)/shard_map/all_to_all | solution.py:445
  46.1 1.2 %collective-permute-start.4 = (f32[3,512]{1,0:T(4,128)S(1)}, f32[3,512]{1,0:T(4,128)S(1)}, u32[]{:S(2)}, u32[]{:S(2)}) collective-permute-start(f32[3,512]{1,0:T(4,128)S(1)} %copy-done.11), channel_id=1, source_target_pairs={{0,4},{4,0},{8,12},{12,8},{16,20},{20,16},{24,28},{28,24},{1,5},{5... | collective-permute-start | bytes 18440 | tf_op jit(solution)/shard_map/ppermute | solution.py:436
  46.3 1.0 %collective-permute-start.5 = (f32[3,512]{1,0:T(4,128)S(1)}, f32[3,512]{1,0:T(4,128)S(1)}, u32[]{:S(2)}, u32[]{:S(2)}) collective-permute-start(f32[3,512]{1,0:T(4,128)S(1)} %copy-done.10), channel_id=1, source_target_pairs={{4,8},{12,16},{20,24},{8,4},{16,12},{24,20},{5,9},{13,17},{21,25},... | collective-permute-start | bytes 18440 | tf_op jit(solution)/shard_map/ppermute | solution.py:437
  47.3 8.1 %copy-start.2 = (f32[3,512]{1,0:T(4,128)}, f32[3,512]{1,0:T(4,128)S(1)}, u32[]{:S(2)}) copy-start(f32[3,512]{1,0:T(4,128)S(1)} %collective-permute-done.4.refs_17_) | copy-start | bytes 18436
  47.3 8.1 %copy-start.3 = (f32[3,512]{1,0:T(4,128)}, f32[3,512]{1,0:T(4,128)S(1)}, u32[]{:S(2)}) copy-start(f32[3,512]{1,0:T(4,128)S(1)} %collective-permute-done.5.refs_18_) | copy-start | bytes 18436

commit v4 on v3

--- a/solution.py
+++ b/solution.py
@@ -515,8 +515,8 @@
             rhs=Held(area),
             q_mixed=Held((rows, cols)),
             partial=area,
-            near=(3 * layers, cols),
-            far=(3 * layers, cols),
+            near=Held((3 * layers, cols)),
+            far=Held((3 * layers, cols)),
             zone_line=Held((1, blocks)),
             chunk=(devices, 1, widths[0]),
         ),
@@ -787,7 +787,7 @@
             ins |= dict(coarse_rows=t.coarse_rows)
         ins |= dict(row_chain=t.row_chain, answer=t.answer, down=t.down, waves=t.waves, own_columns=t.own_columns)
         ins |= dict(around=t.around, wave_weight=t.wave_weight, ends=t.ends, sine_rows=t.sine_rows, weight=t.weight)
-        ins |= dict(sine_cols=t.sine_cols, near=near, far=far, conductivity=conductivity, leakance=leakance, hot=hot)
+        ins |= dict(sine_cols=t.sine_cols, near=Held(near), far=Held(far), conductivity=conductivity, leakance=leakance, hot=hot)
         ins |= shared | more
         ins |= {name: Held(getattr(one, name)) for name in steady} if number else {}
         if number == 2:
@@ -795,7 +795,7 @@
             outs |= dict(chunk=(devices, 1, tail_width))
         else:
             outs = dict(v=area, image=Held(area), q_mixed=Held((rows, cols)))
-            outs |= dict(near=(layers, cols), far=(layers, cols))
+            outs |= dict(near=Held((layers, cols)), far=Held((layers, cols)))
             outs |= dict(chunk=(devices, 1, widths[1]))
         if number == 0:
             outs |= dict(diagonal=area, inverse=area, sides=(layers + 1, rows, 128), beside=(2, cols))

time: 72.5 us -> 72.2 us (level)
  no operation moved by 1% of the time
where the time goes in v4:
time: 72.2 us; the launch traced here: 71.7 us
  waiting for transfers between devices  23.6 us (33%)
  Pallas kernels  22.2 us (31%)
  starting transfers between devices  15.2 us (21%)
  blocking collectives  9.97 us (14%)
  between operations  0.74 us (1%)
    all_to_all x3, waiting for transfers between devices, exchange(): return lax.all_to_all(chunk, BOTH, split_axis=0, concat_axis=0, tiled=True)  22.9 us
    pallas_call x6, Pallas kernels, call(): pl.pallas_call(kernel, out_shape=[pltpu.VMEM(*kind) if isinstance(value,...  22.2 us
    all_to_all x3, starting transfers between devices, exchange(): return lax.all_to_all(chunk, BOTH, split_axis=0, concat_axis=0, tiled=True)  12.5 us
    all_to_all x1, blocking collectives, exchange(): return lax.all_to_all(chunk, BOTH, split_axis=0, concat_axis=0, tiled=True)  9.97 us
    ppermute x3, starting transfers between devices, neighbours(): lax.ppermute(far, 'slab', across + [(j, i) for i, j in across])  1.95 us
  transfers between devices with their start and end apart: 9, of which 5 were waited for; matrix products, arithmetic and copies ran while one was open for 0% of the time, Pallas kernels for 3%

profile of v4, /device:TPU:0, one launch (start us, length us, event | category | flops | bytes accessed | tf_op | source)
XLA Modules:
  0.0 71.7 jit_solution(6511482250261934773)
XLA Ops:
  0.6 3.2 %shard_map.248 = (f32[3,32,512]{2,1,0:T(8,128)S(1)}, f32[32,512]{1,0:T(8,128)S(1)}, f32[3,32,512]{2,1,0:T(8,128)}, f32[9,512]{1,0:T(8,128)S(1)}, f32[9,512]{1,0:...) custom-call(s32[4,64]{1,0:T(4,128)} %refs_0_.1, f32[1,256]{1,0:T(1,128)} %bitcast.6, ...), custom_call_target="tpu_custom_call" | custom-call | tf_op jit(solution)/shard_map/pallas_call | solution.py:392
  3.8 7.3 %all-to-all-start = ((f32[32,1,1920]{2,1,0:T(1,128)}), f32[32,1,1920]{2,1,0:T(1,128)S(1)}, u32[]{:S(2)}, u32[]{:S(2)}) async-start(f32[32,1,1920]{2,1,0:T(1,128)} %get-tuple-element.42), calls=%async_computation | async-start | bytes 491520 | tf_op jit(solution)/shard_map/all_to_all | solution.py:445
  11.2 0.3 collective-permute-start
  11.5 0.7 collective-permute-start.1
  12.1 2.3 %shard_map.249 = (f32[256,256]{1,0:T(8,128)}, bf16[256,256]{1,0:T(8,128)(2,1)}) custom-call(s32[2,512]{1,0:T(2,128)} %bitcast.4, f32[1,512]{1,0:T(1,128)} %bitcast.5, f32[1,256]{1,0:T(1,128)} %bitcast.7, f32[1,256]{1,0:T(1,128)S(1)} %get-tuple-element.45.refs_3_.refs_1_), custom_call_target="tpu_custom_call" | custom-call | tf_op jit(solution)/shard_map/pallas_call | solution.py:392
  14.4 0.0 collective-permute-done.refs_12_
  14.4 0.0 collective-permute-done.1.refs_13_
  14.4 6.7 %all-to-all-done.refs_0_ = f32[32,1,1920]{2,1,0:T(1,128)S(1)} async-done(((f32[32,1,1920]{2,1,0:T(1,128)}), f32[32,1,1920]{2,1,0:T(1,128)S(1)}, u32[]{:S(2)}, u32[]{:S(2)}) %all-to-all-start) | async-done | bytes 245792 | tf_op jit(solution)/shard_map/all_to_all | solution.py:445
  21.2 4.8 %shard_map.250 = (f32[3,32,512]{2,1,0:T(8,128)}, f32[3,32,512]{2,1,0:T(8,128)S(1)}, f32[32,512]{1,0:T(8,128)S(1)}, f32[3,512]{1,0:T(4,128)S(1)}, f32[3,512]{1,0:...) custom-call(f32[32,1,1920]{2,1,0:T(1,128)S(1)} %all-to-all-done.refs, ...), custom_call_target="tpu_custom_call" | custom-call | tf_op jit(solution)/shard_map/pallas_call | solution.py:392
  26.0 2.6 %all-to-all-start.1 = ((f32[32,1,1536]{2,1,0:T(1,128)}), f32[32,1,1536]{2,1,0:T(1,128)S(1)}, u32[]{:S(2)}, u32[]{:S(2)}) async-start(f32[32,1,1536]{2,1,0:T(1,128)} %get-tuple-element.50), calls=%async_computation.1 | async-start | bytes 393216 | tf_op jit(solution)/shard_map/all_to_all | solution.py:445
  28.6 0.3 collective-permute-start.2
  28.9 0.6 collective-permute-start.3
  29.5 0.3 collective-permute-done.2.refs_17_
  29.8 0.0 collective-permute-done.3.refs_18_
  29.8 8.1 %all-to-all-done.1.refs_0_ = f32[32,1,1536]{2,1,0:T(1,128)S(1)} async-done(((f32[32,1,1536]{2,1,0:T(1,128)}), f32[32,1,1536]{2,1,0:T(1,128)S(1)}, u32[]{:S(2)}, u32[]{:S(2)}) %all-to-all-start.1) | async-done | bytes 196640 | tf_op jit(solution)/shard_map/all_to_all | solution.py:445
  37.9 5.4 %shard_map.251 = (f32[3,32,512]{2,1,0:T(8,128)}, f32[3,32,512]{2,1,0:T(8,128)S(1)}, f32[32,512]{1,0:T(8,128)S(1)}, f32[3,512]{1,0:T(4,128)S(1)}, f32[3,512]{1,0:...) custom-call(f32[32,1,1536]{2,1,0:T(1,128)S(1)} %all-to-all-done.1.refs_0_, ...), custom_call_target="tpu_custom_call" | custom-call | tf_op jit(solution)/shard_map/pallas_call | solution.py:392
  43.3 2.6 %all-to-all-start.2 = ((f32[32,1,1536]{2,1,0:T(1,128)}), f32[32,1,1536]{2,1,0:T(1,128)S(1)}, u32[]{:S(2)}, u32[]{:S(2)}) async-start(f32[32,1,1536]{2,1,0:T(1,128)} %get-tuple-element.65), calls=%async_computation.2 | async-start | bytes 393216 | tf_op jit(solution)/shard_map/all_to_all | solution.py:445
  45.9 0.2 collective-permute-start.4
  46.1 0.6 collective-permute-start.5
  46.7 0.4 collective-permute-done.4.refs_17_
  47.1 8.1 %all-to-all-done.2.refs_0_ = f32[32,1,1536]{2,1,0:T(1,128)S(1)} async-done(((f32[32,1,1536]{2,1,0:T(1,128)}), f32[32,1,1536]{2,1,0:T(1,128)S(1)}, u32[]{:S(2)}, u32[]{:S(2)}) %all-to-all-start.2) | async-done | bytes 196640 | tf_op jit(solution)/shard_map/all_to_all | solution.py:445
  55.2 4.8 %shard_map.252 = (f32[3,32,512]{2,1,0:T(8,128)S(1)}, f32[3,32,512]{2,1,0:T(8,128)S(1)}, f32[3,32,512]{2,1,0:T(8,128)S(1)}, f32[32,1,384]{2,1,0:T(1,128)}, f32[3,...) custom-call(f32[32,1,1536]{2,1,0:T(1,128)S(1)} %all-to-all-done.2.re, ...), custom_call_target="tpu_custom_call" | custom-call | tf_op jit(solution)/shard_map/pallas_call | solution.py:392
  60.1 10.0 %all_to_all.20.refs_0_ = f32[32,1,384]{2,1,0:T(1,128)S(1)} all-to-all(f32[32,1,384]{2,1,0:T(1,128)} %get-tuple-element.73), channel_id=1, replica_groups=mesh['slab'=8,'grp'=4] {'slab','grp'}, dimensions={0} | all-to-all | bytes 98304 | tf_op jit(solution)/shard_map/all_to_all | solution.py:445
  70.0 1.7 %shard_map.253 = (f32[3,32,512]{2,1,0:T(8,128)}, f32[3,32,512]{2,1,0:T(8,128)}) custom-call(f32[32,1,384]{2,1,0:T(1,128)S(1)} %all_to_all.20.refs_0_, f32[1,256]{1,0:T(1,128)S(1)} %get-tuple-element.45.refs_3_.refs_1_, f32[3,32,512]{2,1,0:T(8,128)S(1)} %get-tuple-element.49.refs_19_.refs_30_.refs_2_, f32[3,32,512]{2,1,0:T(8,128)S(1)} %get-tuple-element.74.refs_3_, ...), custom_call_target="tpu_custom_call" | custom-call | tf_op jit(solution)/shard_map/pallas_call | solution.py:392
  (1 shorter events, 0.0 us)
Async XLA Ops:
  3.8 17.3 %all-to-all-start = ((f32[32,1,1920]{2,1,0:T(1,128)}), f32[32,1,1920]{2,1,0:T(1,128)S(1)}, u32[]{:S(2)}, u32[]{:S(2)}) async-start(f32[32,1,1920]{2,1,0:T(1,128)} %get-tuple-element.42), calls=%async_computation | async-start | bytes 491520 | tf_op jit(solution)/shard_map/all_to_all | solution.py:445
  11.2 3.2 %collective-permute-start = (f32[9,512]{1,0:T(8,128)S(1)}, f32[9,512]{1,0:T(8,128)S(1)}, u32[]{:S(2)}, u32[]{:S(2)}) collective-permute-start(f32[9,512]{1,0:T(8,128)S(1)} %get-tuple-element.43), channel_id=1, source_target_pairs={{0,4},{4,0},{8,12},{12,8},{16,20},{20,16},{24,28},{28,24},{1,5},{5... | collective-permute-start | bytes 55304 | tf_op jit(solution)/shard_map/ppermute | solution.py:436
  11.5 2.9 %collective-permute-start.1 = (f32[9,512]{1,0:T(8,128)S(1)}, f32[9,512]{1,0:T(8,128)S(1)}, u32[]{:S(2)}, u32[]{:S(2)}) collective-permute-start(f32[9,512]{1,0:T(8,128)S(1)} %get-tuple-element.44), channel_id=1, source_target_pairs={{4,8},{12,16},{20,24},{8,4},{16,12},{24,20},{5,9},{13,17},{21,25},... | collective-permute-start | bytes 55304 | tf_op jit(solution)/shard_map/ppermute | solution.py:437
  26.0 11.9 %all-to-all-start.1 = ((f32[32,1,1536]{2,1,0:T(1,128)}), f32[32,1,1536]{2,1,0:T(1,128)S(1)}, u32[]{:S(2)}, u32[]{:S(2)}) async-start(f32[32,1,1536]{2,1,0:T(1,128)} %get-tuple-element.50), calls=%async_computation.1 | async-start | bytes 393216 | tf_op jit(solution)/shard_map/all_to_all | solution.py:445
  28.6 1.2 %collective-permute-start.2 = (f32[3,512]{1,0:T(4,128)S(1)}, f32[3,512]{1,0:T(4,128)S(1)}, u32[]{:S(2)}, u32[]{:S(2)}) collective-permute-start(f32[3,512]{1,0:T(4,128)S(1)} %get-tuple-element.55), channel_id=1, source_target_pairs={{0,4},{4,0},{8,12},{12,8},{16,20},{20,16},{24,28},{28,24},{1,5},{5... | collective-permute-start | bytes 18440 | tf_op jit(solution)/shard_map/ppermute | solution.py:436
  28.9 0.9 %collective-permute-start.3 = (f32[3,512]{1,0:T(4,128)S(1)}, f32[3,512]{1,0:T(4,128)S(1)}, u32[]{:S(2)}, u32[]{:S(2)}) collective-permute-start(f32[3,512]{1,0:T(4,128)S(1)} %get-tuple-element.56), channel_id=1, source_target_pairs={{4,8},{12,16},{20,24},{8,4},{16,12},{24,20},{5,9},{13,17},{21,25},... | collective-permute-start | bytes 18440 | tf_op jit(solution)/shard_map/ppermute | solution.py:437
  43.3 11.9 %all-to-all-start.2 = ((f32[32,1,1536]{2,1,0:T(1,128)}), f32[32,1,1536]{2,1,0:T(1,128)S(1)}, u32[]{:S(2)}, u32[]{:S(2)}) async-start(f32[32,1,1536]{2,1,0:T(1,128)} %get-tuple-element.65), calls=%async_computation.2 | async-start | bytes 393216 | tf_op jit(solution)/shard_map/all_to_all | solution.py:445
  45.9 1.2 %collective-permute-start.4 = (f32[3,512]{1,0:T(4,128)S(1)}, f32[3,512]{1,0:T(4,128)S(1)}, u32[]{:S(2)}, u32[]{:S(2)}) collective-permute-start(f32[3,512]{1,0:T(4,128)S(1)} %get-tuple-element.66), channel_id=1, source_target_pairs={{0,4},{4,0},{8,12},{12,8},{16,20},{20,16},{24,28},{28,24},{1,5},{5... | collective-permute-start | bytes 18440 | tf_op jit(solution)/shard_map/ppermute | solution.py:436
  46.1 1.1 %collective-permute-start.5 = (f32[3,512]{1,0:T(4,128)S(1)}, f32[3,512]{1,0:T(4,128)S(1)}, u32[]{:S(2)}, u32[]{:S(2)}) collective-permute-start(f32[3,512]{1,0:T(4,128)S(1)} %get-tuple-element.67), channel_id=1, source_target_pairs={{4,8},{12,16},{20,24},{8,4},{16,12},{24,20},{5,9},{13,17},{21,25},... | collective-permute-start | bytes 18440 | tf_op jit(solution)/shard_map/ppermute | solution.py:437
